TPU v7x, 256 devices: a whole 4x4x8 slice. The times are simulated.
256 devices in a mesh: row: 16 (over x, y), col: 16 (over z, core).
Axes of the slice: x: 4, y: 4, z: 8, core: 2. Of those that a mesh axis runs over, the one named last changes fastest.
Arguments:
- tokens: bfloat16 [2048, 8192], P('col', 'row'), may hold values from -6 to 6
- grad_out: bfloat16 [2048, 8192], P('col', 'row'), may hold values from -0.59765625 to 0.59765625
- gate_weight: bfloat16 [8192, 14336], P('row', 'col'), may hold values from -0.09375 to 0.09375
- up_weight: bfloat16 [8192, 14336], P('row', 'col'), may hold values from -0.09375 to 0.09375
- down_weight: bfloat16 [14336, 8192], P('col', 'row'), may hold values from -0.0625 to 0.0625
- gate_mask: int32 [64, 112], P('row', 'col'), may hold values from 0 to 1, as said below
- up_mask: int32 [64, 112], P('row', 'col'), may hold values from 0 to 1, as said below
- down_mask: int32 [112, 64], P('col', 'row'), may hold values from 0 to 1, as said below
Outputs:
- layer_output: bfloat16 [2048, 8192], P('col', 'row')
- input_grad: bfloat16 [2048, 8192], P('col', 'row')
- gate_grad: bfloat16 [8192, 14336], P('row', 'col')
- up_grad: bfloat16 [8192, 14336], P('row', 'col')
- down_grad: bfloat16 [14336, 8192], P('col', 'row')
Inputs may be any that keep to these rules, and one draw needn't show every extreme that they name: `gate_mask`: 1 marks a live block of 128 x 128 weights, 0 a pruned one. `up_mask`: 1 marks a live block of 128 x 128 weights, 0 a pruned one. `down_mask`: 1 marks a live block of 128 x 128 weights, 0 a pruned one.
All inputs are finite; a program needn't handle non-finite values.
Results may differ from a plain program's by a relative error of at most 0.035.
Values may be sent and summed in bfloat16 or wider, within the bound.
A program may use at most 128 MiB of HBM per device.

v0:
```python
import jax
import jax.numpy as jnp
from jax import lax
from jax.sharding import PartitionSpec as P

BLK = 128


def expand_mask(mask_tile, weight_tile):
    blocks_a, blocks_b = mask_tile.shape
    scaled = mask_tile.astype(weight_tile.dtype)[:, None, :, None]
    return (weight_tile.reshape(blocks_a, BLK, blocks_b, BLK) * scaled).reshape(weight_tile.shape)


def activation_parts(gate_up, width):
    gate_act = gate_up[:, :width].astype(jnp.float32)
    sigmoid_g = jax.nn.sigmoid(gate_act)
    silu_g = gate_act * sigmoid_g
    slope_g = sigmoid_g * (1.0 + gate_act * (1.0 - sigmoid_g))
    return (silu_g, slope_g)


def combine_grads(hidden_grad, gate_up, silu_g, slope_g, width):
    up_act = gate_up[:, width:].astype(jnp.float32)
    gate_act_grad = (hidden_grad * up_act * slope_g).astype(jnp.bfloat16)
    up_act_grad = (hidden_grad * silu_g).astype(jnp.bfloat16)
    return jnp.concatenate((gate_act_grad, up_act_grad), 1)


def body(tokens, grad_out, gate_weight, up_weight, down_weight, gate_mask, up_mask, down_mask):
    token_cols, grad_cols = (
        lax.all_gather(tokens, "col", axis=0, tiled=True),
        lax.all_gather(grad_out, "col", axis=0, tiled=True),
    )
    width = gate_weight.shape[1]
    gate_up_w = jnp.concatenate(
        (expand_mask(gate_mask, gate_weight), expand_mask(up_mask, up_weight)), 1
    )
    down_w = expand_mask(down_mask, down_weight)
    gate_up = lax.psum_scatter(
        jnp.dot(token_cols, gate_up_w, preferred_element_type=jnp.float32).astype(jnp.bfloat16),
        "row",
        scatter_dimension=0,
        tiled=True,
    )
    silu_own, slope_own = activation_parts(gate_up, width)
    hidden_own = (silu_own * gate_up[:, width:].astype(jnp.float32)).astype(jnp.bfloat16)
    hidden_all = lax.all_gather(hidden_own, "row", axis=0, tiled=True)
    layer_output = lax.psum_scatter(
        jnp.dot(hidden_all, down_w, preferred_element_type=jnp.float32).astype(jnp.bfloat16),
        "col",
        scatter_dimension=0,
        tiled=True,
    )
    down_full = lax.dot_general(
        hidden_all, grad_cols, (((0,), (0,)), ((), ())), preferred_element_type=jnp.float32
    )
    down_grad = expand_mask(down_mask, down_full).astype(jnp.bfloat16)
    grad_rows = grad_cols
    hidden_grad = lax.psum_scatter(
        lax.dot_general(
            grad_rows, down_w, (((1,), (1,)), ((), ())), preferred_element_type=jnp.float32
        ).astype(jnp.bfloat16),
        "row",
        scatter_dimension=0,
        tiled=True,
    ).astype(jnp.float32)
    grads_own = combine_grads(hidden_grad, gate_up, silu_own, slope_own, width)
    grads_all = lax.all_gather(grads_own, "row", axis=0, tiled=True)
    weight_grads = lax.dot_general(
        token_cols, grads_all, (((0,), (0,)), ((), ())), preferred_element_type=jnp.float32
    )
    gate_grad = expand_mask(gate_mask, weight_grads[:, :width]).astype(jnp.bfloat16)
    up_grad = expand_mask(up_mask, weight_grads[:, width:]).astype(jnp.bfloat16)
    grad_rows = grads_all
    input_grad = lax.psum_scatter(
        lax.dot_general(
            grad_rows, gate_up_w, (((1,), (1,)), ((), ())), preferred_element_type=jnp.float32
        ).astype(jnp.bfloat16),
        "col",
        scatter_dimension=0,
        tiled=True,
    )
    return (layer_output, input_grad, gate_grad, up_grad, down_grad)


def solution(mesh):
    placed = (
        P("col", "row"),
        P("col", "row"),
        P("row", "col"),
        P("row", "col"),
        P("col", "row"),
        P("row", "col"),
        P("row", "col"),
        P("col", "row"),
    )
    return jax.shard_map(
        body,
        mesh=mesh,
        in_specs=placed,
        out_specs=(
            P("col", "row"),
            P("col", "row"),
            P("row", "col"),
            P("row", "col"),
            P("col", "row"),
        ),
        check_vma=False,
    )
```

profile of v0, /device:TPU:32, one launch (start us, length us, event | category | flops | bytes accessed | tf_op | source)
XLA Modules:
  0.0 535.8 jit_solution(5050220587588536091)
XLA Ops:
  7.2 0.7 all-gather.9.cloned.1.call-update
  7.9 0.7 all-gather.5.cloned.1.call-update
  8.7 0.8 fusion.16
  9.5 0.1 copy.33
  9.6 41.9 %all-gather.9.cloned.1.call-done = bf16[2048,512]{1,0:T(8,128)(2,1)} async-done(((bf16[128,512]{1,0:T(8,128)(2,1)}), bf16[2048,512]{1,0:T(8,128)(2,1)}) %all-gather.9.cloned.1.call-update) | async-done | bytes 2097168 | tf_op jit(solution)/shard_map/all_gather | solution.py:33
  51.5 0.3 mul.95
  51.8 0.9 copy-done.2
  52.7 5.8 %convert_bitcast_fusion = bf16[2048,896]{0,1:T(8,128)(2,1)} fusion(bf16[2048,512]{1,0:T(8,128)(2,1)} %all-gather.9.cloned.1.call-done, bf16[896,512]{1,0:T(8,128)(2,1)} %param.12, bf16[112,8,4,128]{3,2,1,0:T(4,128)(2,1)S(1)} %bitcast.61), kind=kOutput, calls=%fused_computation.2 | convolution fusion | flops 1881341952 | bytes 7602176 | tf_op jit(solution)/shard_map/dot_general | solution.py:61
  58.5 6.1 %copy.41 = bf16[2048,896]{1,0:T(8,128)(2,1)} copy(bf16[2048,896]{0,1:T(8,128)(2,1)} %convert_bitcast_fusion) | data formatting | bytes 7340032
  64.6 0.6 copy-done.5
  65.2 0.1 copy.31
  65.4 0.1 copy.29
  65.5 0.3 copy-done
  65.8 0.5 copy.30
  66.3 0.5 copy.32
  66.8 0.3 mul.90
  67.2 0.3 mul.87
  67.5 1.2 bitcast_multiply_fusion.4
  68.7 22.7 %all-gather.5.cloned.1.call-done = bf16[2048,512]{1,0:T(8,128)(2,1)} async-done(((bf16[128,512]{1,0:T(8,128)(2,1)}), bf16[2048,512]{1,0:T(8,128)(2,1)}) %all-gather.5.cloned.1.call-update) | async-done | bytes 2097168 | tf_op jit(solution)/shard_map/all_gather | solution.py:32
  91.4 8.9 %fusion = bf16[2048,1792]{0,1:T(8,128)(2,1)} fusion(bf16[2048,512]{1,0:T(8,128)(2,1)} %all-gather.5.cloned.1.call-done, bf16[512,896]{0,1:T(8,128)(2,1)S(1)} %get-tuple-element.33, bf16[512,896]{0,1:T(8,128)(2,1)} %get-tuple-element.34), kind=kOutput, calls=%fused_computation.1 | convolution fusion | flops 3765436416 | bytes 11272192 | tf_op jit(solution)/shard_map/dot_general | solution.py:41
  100.2 10.1 %copy.39 = bf16[2048,1792]{1,0:T(8,128)(2,1)} copy(bf16[2048,1792]{0,1:T(8,128)(2,1)} %fusion) | data formatting | bytes 14680064
  110.4 65.1 %reduce-scatter.15.cloned.1.call-done = bf16[128,896]{1,0:T(8,128)(2,1)} async-done(((bf16[2048,896]{1,0:T(8,128)(2,1)}), bf16[128,896]{1,0:T(8,128)(2,1)}) %reduce-scatter.15.cloned.1.call-update) | async-done | bytes 229392
  175.6 1.1 copy.42
  176.7 89.7 %reduce-scatter.13.cloned.1.call-done = bf16[128,1792]{1,0:T(8,128)(2,1)} async-done(((bf16[2048,1792]{1,0:T(8,128)(2,1)}), bf16[128,1792]{1,0:T(8,128)(2,1)}) %reduce-scatter.13.cloned.1.call-update) | async-done | bytes 458768
  266.4 1.1 fusion.15
  267.5 0.2 copy.43
  267.7 0.2 copy.44
  267.8 1.0 fusion.6
  268.9 0.8 pad_maximum_fusion.3
  269.8 58.7 %all-gather.7.cloned.1.call-done = bf16[2048,896]{0,1:T(8,128)(2,1)} async-done(((bf16[128,896]{0,1:T(8,128)(2,1)}), bf16[2048,896]{0,1:T(8,128)(2,1)}) %all-gather.7.cloned.1.call-update) | async-done | bytes 3670032 | tf_op jit(solution)/shard_map/all_gather | solution.py:48
  328.5 6.1 %convolution_convert_fusion.1 = bf16[2048,512]{1,0:T(8,128)(2,1)} fusion(bf16[2048,896]{0,1:T(8,128)(2,1)} %all-gather.7.cloned.1.call-done, bf16[896,512]{1,0:T(8,128)(2,1)} %param.12, bf16[112,8,4,128]{3,2,1,0:T(4,128)(2,1)S(1)} %bitcast.62), kind=kOutput, calls=%fused_computation.4 | convolution fusion | flops 1880555520 | bytes 7602176 | tf_op jit(solution)/shard_map/dot_general | solution.py:50
  334.6 0.2 reduce-scatter.11.cloned.1.call-start
  334.8 74.3 %all-gather.11.cloned.1.call-done = bf16[2048,1792]{0,1:T(8,128)(2,1)} async-done(((bf16[128,1792]{0,1:T(8,128)(2,1)}), bf16[2048,1792]{0,1:T(8,128)(2,1)}) %all-gather.11.cloned.1.call-update) | async-done | bytes 7340048 | tf_op jit(solution)/shard_map/all_gather | solution.py:69
  409.1 8.5 %convolution_convert_fusion.2 = bf16[2048,512]{1,0:T(8,128)(2,1)} fusion(bf16[2048,1792]{0,1:T(8,128)(2,1)} %all-gather.11.cloned.1.call-done, bf16[512,896]{0,1:T(8,128)(2,1)S(1)} %get-tuple-element.33, bf16[512,896]{0,1:T(8,128)(2,1)S(1)} %copy-done.4), kind=kOutput, calls=%fused_computation.5 | convolution fusion | flops 3762814976 | bytes 11272192 | tf_op jit(solution)/shard_map/dot_general | solution.py:77
  417.7 0.1 copy.34
  417.8 0.1 copy.35
  417.9 0.1 copy.36
  418.0 0.3 mul.109
  418.3 1.0 copy-done.7
  419.2 5.3 fusion.1
  424.6 4.0 convolution_bitcast_fusion
  428.5 0.3 mul.103
  428.8 0.3 mul.106
  429.2 1.0 fusion.2
  430.2 1.3 copy.37
  431.5 1.3 copy.38
  432.7 35.1 %reduce-scatter.9.cloned.1.call-done = bf16[128,512]{1,0:T(8,128)(2,1)} async-done(((bf16[2048,512]{1,0:T(8,128)(2,1)}), bf16[128,512]{1,0:T(8,128)(2,1)}) %reduce-scatter.9.cloned.1.call-update) | async-done | bytes 131088 | tf_op jit(solution)/shard_map/reduce_scatter | solution.py:49
  467.8 61.1 %reduce-scatter.11.cloned.1.call-done = bf16[128,512]{1,0:T(8,128)(2,1)} async-done(((bf16[2048,512]{1,0:T(8,128)(2,1)}), bf16[128,512]{1,0:T(8,128)(2,1)}) %reduce-scatter.11.cloned.1.call-update) | async-done | bytes 131088 | tf_op jit(solution)/shard_map/reduce_scatter | solution.py:76
  (34 shorter events, 0.4 us)
Async XLA Ops:
  7.2 44.3 %all-gather.9.cloned.1.call-start = ((), (), s32[]{:S(2)}) async-start(), calls=%async_computation.7 | async-start | bytes 2228224 | tf_op jit(solution)/shard_map/all_gather | solution.py:33
  7.9 83.5 %all-gather.5.cloned.1.call-start = ((), (), s32[]{:S(2)}) async-start(), calls=%async_computation.4 | async-start | bytes 2228224 | tf_op jit(solution)/shard_map/all_gather | solution.py:32
  8.6 166.9 %reduce-scatter.15.cloned.1.call-start = ((), (), s32[]{:S(2)}) async-start(), calls=%async_computation.11 | async-start | bytes 3899392
  51.8 0.9 copy-start.2
  64.6 0.7 copy-start.5
  64.6 0.8 copy-start.6
  64.6 1.2 copy-start
  64.6 1.7 copy-start.1
  64.6 201.8 %reduce-scatter.13.cloned.1.call-start = ((), (), s32[]{:S(2)}) async-start(), calls=%async_computation.10 | async-start | bytes 7798784
  110.4 218.1 %all-gather.7.cloned.1.call-start = ((), (), s32[]{:S(2)}) async-start(), calls=%async_computation.5 | async-start | bytes 3899392 | tf_op jit(solution)/shard_map/all_gather | solution.py:48
  267.5 61.0 %copy-start.3 = (bf16[7,128,4,128]{3,2,1,0:T(4,128)(2,1)S(1)}, bf16[7,128,4,128]{3,2,1,0:T(4,128)(2,1)}, u32[]{:S(2)}) copy-start(bf16[7,128,4,128]{3,2,1,0:T(4,128)(2,1)} %copy-done.2) | copy-start | bytes 2752516
  268.9 140.2 %all-gather.11.cloned.1.call-start = ((), (), s32[]{:S(2)}) async-start(), calls=%async_computation.8 | async-start | bytes 7798784 | tf_op jit(solution)/shard_map/all_gather | solution.py:69
  269.7 198.1 %reduce-scatter.9.cloned.1.call-start = ((), (), s32[]{:S(2)}) async-start(), calls=%async_computation.6 | async-start | bytes 2228224 | tf_op jit(solution)/shard_map/reduce_scatter | solution.py:49
  334.5 74.6 %copy-start.4 = (bf16[512,896]{0,1:T(8,128)(2,1)S(1)}, bf16[512,896]{0,1:T(8,128)(2,1)}, u32[]{:S(2)}) copy-start(bf16[512,896]{0,1:T(8,128)(2,1)} %get-tuple-element.34) | copy-start | bytes 2752516
  334.6 194.3 %reduce-scatter.11.cloned.1.call-start = ((), (), s32[]{:S(2)}) async-start(), calls=%async_computation.9 | async-start | bytes 2228224 | tf_op jit(solution)/shard_map/reduce_scatter | solution.py:76
  417.6 1.6 copy-start.7
  418.0 6.6 %slice-start = ((s8[7340032]{0:T(1024)(128)(4,1)}), s8[4194304]{0:T(1024)(128)(4,1)S(1)}, s32[]{:S(2)}) async-start(s8[7340032]{0:T(1024)(128)(4,1)} %bitcast.63), calls=%async_computation.12 | async-start | bytes 8388608
  419.2 5.3 slice-start.1
  419.2 5.3 copy-start.8
Sparse Core Ops, SparseCore 0:
  9.8 41.5 all-gather.8
  53.3 38.0 all-gather.4
  95.0 80.4 reduce-scatter.14
  179.2 87.1 reduce-scatter.12
  269.0 59.4 all-gather.6
  331.6 77.4 all-gather.10
  412.4 55.4 reduce-scatter.8
  471.1 57.7 reduce-scatter.10
where the time goes:
time: 540 us; the launch traced here: 536 us
  waiting for transfers between devices  450 us (83%)
  matrix products  38.5 us (7%)
  local copies, waits for them, and re-layouts  27.5 us (5%)
  between operations  14.3 us (3%)
    unnamed x10, waiting for transfers between devices  156 us
    all_gather x1, waiting for transfers between devices, body(): grads_all = lax.all_gather(grads_own, 'row', axis=0, tiled=True)  74.3 us
    reduce_scatter x1, waiting for transfers between devices, body(): lax.psum_scatter(lax.dot_general(grad_rows, gate_up_w, (((1,), (1,)), (()...  61.1 us
    all_gather x1, waiting for transfers between devices, body(): hidden_all = lax.all_gather(hidden_own, 'row', axis=0, tiled=True)  58.7 us
    all_gather x1, waiting for transfers between devices, body(): lax.all_gather(grad_out, 'col', axis=0, tiled=True)  41.9 us
    reduce_scatter x1, waiting for transfers between devices, body(): lax.psum_scatter(jnp.dot(hidden_all, down_w, preferred_element_type=jnp.f...  35.1 us
    unnamed x31, local copies, waits for them, and re-layouts  24 us
    all_gather x1, waiting for transfers between devices, body(): lax.all_gather(tokens, 'col', axis=0, tiled=True)  22.7 us
  transfers between devices with their start and end apart: 8, of which 8 were waited for; matrix products, arithmetic and copies ran while one was open for 12% of the time, Pallas kernels for 0%

commit v1 on v0

v1 whole, which is shorter than its diff:
```python
import jax
import jax.numpy as jnp
from jax import lax
from jax.experimental import pallas as pl
from jax.experimental.pallas import tpu as pltpu
from jax.sharding import PartitionSpec as P

BLK = 128
NX, NY, NZ = 4, 4, 8
F = 896
D = 512
F32, BF = jnp.float32, jnp.bfloat16
MESH = pl.DeviceIdType.MESH
NSEM = 200


def rows_of(ref, *lead):
    value = ref[lead]
    return value.reshape(256, value.shape[-1])


def dot_nn(a, b):
    return jnp.dot(a, b, preferred_element_type=F32)


def dot_nt(a, b):
    return lax.dot_general(a, b, (((1,), (1,)), ((), ())), preferred_element_type=F32)


class Link:
    def __init__(self, send_sem, recv_sem):
        self.send_sem, self.recv_sem, self.copies = send_sem, recv_sem, []

    def send(self, src, dst, device):
        at = len(self.copies)
        copy = pltpu.make_async_remote_copy(
            src_ref=src, dst_ref=dst, send_sem=self.send_sem.at[at], recv_sem=self.recv_sem.at[at],
            device_id=device, device_id_type=MESH,
        )
        copy.start()
        self.copies.append(copy)
        return copy

    def drain(self):
        for copy in self.copies:
            copy.wait_send()


class GatherZ:
    def __init__(self, link, where, full, own):
        self.link, self.w, self.full, self.own = link, where, full, own

    def slot(self, k, *half):
        chunk = lax.rem(self.w.z + k + NZ, NZ) * 2 + self.w.core
        return self.full.at[(lax.div(chunk, 4), lax.rem(chunk, 4), *half)]

    def start(self):
        own = self.slot(0)
        own[...] = self.own[...]
        self.right = [self.link.send(own, own, self.w.Z(1))]
        self.left = [self.link.send(own, own, self.w.Z(-1))]
        self.side = [self.link.send(own, own, self.w.sibling)]

    def step(self, k):
        for copies, sign, half in ((self.right, -1, 0), (self.left, 1, 1)):
            copies[k - 1].wait_recv()
            got = self.slot(sign * k)
            on = got if k < 3 else self.slot(sign * k, half)
            copies.append(self.link.send(on, on, self.w.Z(-sign)))
            self.side.append(self.link.send(got, got, self.w.sibling))

    def last(self):
        self.right[3].wait_recv()
        self.left[3].wait_recv()
        got = self.slot(4)
        self.side.append(self.link.send(got, got, self.w.sibling))

    def finish(self):
        for copy in self.side:
            copy.wait_recv()


class ScatterXY:
    def __init__(self, link, where, half, full, bufs):
        self.link, self.half, self.full = link, half, full
        self.r1, self.r2, self.s, self.q1, self.q2 = bufs
        if half == 0:
            self.m, self.o, self.first, self.second = where.x, where.y, where.X, where.Y
        else:
            self.m, self.o, self.first, self.second = where.y, where.x, where.Y, where.X

    def index(self, k, *other):
        d = lax.rem(self.m + k + 4, 4)
        o = other[0] if other else slice(None)
        return (d, o, self.half) if self.half == 0 else (o, d, self.half)

    def opposite(self):
        lo, hi = (self.full.at[self.index(2, slice(a, a + 2))] for a in (0, 2))
        self.a_p = self.link.send(lo, self.r1.at[0], self.first(1))
        self.a_m = self.link.send(hi, self.r1.at[1], self.first(-1))

    def raw(self):
        hi = self.full.at[self.index(1, slice(2, 4))]
        lo = self.full.at[self.index(-1, slice(0, 2))]
        self.b_p = self.link.send(hi, self.r2.at[0, 2:4], self.first(1))
        self.b_m = self.link.send(lo, self.r2.at[1, 0:2], self.first(-1))

    def sums(self):
        self.a_p.wait_recv()
        for i in range(2):
            at = self.index(1, i)
            self.full[at] = (self.full[at].astype(F32) + self.r1[0, i].astype(F32)).astype(BF)
        src = self.full.at[self.index(1, slice(0, 2))]
        self.c_p = self.link.send(src, self.r2.at[0, 0:2], self.first(1))
        self.a_m.wait_recv()
        for i in range(2):
            at = self.index(-1, i + 2)
            self.full[at] = (self.full[at].astype(F32) + self.r1[1, i].astype(F32)).astype(BF)
        src = self.full.at[self.index(-1, slice(2, 4))]
        self.c_m = self.link.send(src, self.r2.at[1, 2:4], self.first(-1))

    def middle(self):
        for copy in (self.b_p, self.b_m, self.c_p, self.c_m):
            copy.wait_recv()
        for k in (2, 1, 3, 0):
            i = lax.rem(self.o + k, 4)
            at = self.index(0, i)
            self.s[i] = (
                self.full[at].astype(F32) + self.r2[0, i].astype(F32) + self.r2[1, i].astype(F32)
            ).astype(BF)
        p, q, m = (lax.rem(self.o + k, 4) for k in (1, 2, 3))
        self.d_p = self.link.send(self.s.at[q, 0:32], self.q1.at[0], self.second(1))
        self.d_m = self.link.send(self.s.at[q, 32:64], self.q1.at[1], self.second(-1))
        self.e_p = self.link.send(self.s.at[p, 32:64], self.q2.at[0, 32:64], self.second(1))
        self.e_m = self.link.send(self.s.at[m, 0:32], self.q2.at[1, 0:32], self.second(-1))

    def sums2(self):
        p, m = (lax.rem(self.o + k, 4) for k in (1, 3))
        self.d_p.wait_recv()
        self.s[p, 0:32] = (self.s[p, 0:32].astype(F32) + self.q1[0].astype(F32)).astype(BF)
        self.f_p = self.link.send(self.s.at[p, 0:32], self.q2.at[0, 0:32], self.second(1))
        self.d_m.wait_recv()
        self.s[m, 32:64] = (self.s[m, 32:64].astype(F32) + self.q1[1].astype(F32)).astype(BF)
        self.f_m = self.link.send(self.s.at[m, 32:64], self.q2.at[1, 32:64], self.second(-1))

    def arrive(self):
        for copy in (self.e_p, self.e_m, self.f_p, self.f_m):
            copy.wait_recv()

    def result(self, cols):
        return (
            self.s[self.o, :, cols].astype(F32)
            + self.q2[0, :, cols].astype(F32)
            + self.q2[1, :, cols].astype(F32)
        )


class GatherXY:
    def __init__(self, link, where, half, full):
        self.link, self.half, self.full = link, half, full
        if half == 0:
            self.m, self.o, self.first, self.second = where.x, where.y, where.X, where.Y
        else:
            self.m, self.o, self.first, self.second = where.y, where.x, where.Y, where.X
        self.p, self.q = [], []

    def at(self, k, j, *rows):
        a, b = lax.rem(self.m + k + 4, 4), lax.rem(self.o + j + 4, 4)
        return self.full.at[(a, b, self.half, *rows) if self.half == 0 else (b, a, self.half, *rows)]

    def send(self, ref, device):
        return self.link.send(ref, ref, device)

    def across(self, k):
        piece = self.at(k, 0)
        self.p.append(self.send(piece, self.second(1)))
        self.q.append(self.send(piece, self.second(-1)))

    def start(self):
        piece = self.at(0, 0)
        self.a_p = self.send(piece, self.first(1))
        self.a_m = self.send(piece, self.first(-1))
        self.across(0)

    def near(self):
        self.a_p.wait_recv()
        self.b_p = self.send(self.at(-1, 0, slice(0, 32)), self.first(1))
        self.a_m.wait_recv()
        self.b_m = self.send(self.at(1, 0, slice(32, 64)), self.first(-1))
        self.across(-1)
        self.across(1)

    def far(self):
        self.b_p.wait_recv()
        self.b_m.wait_recv()
        self.across(2)

    def relay(self, n):
        k = (0, -1, 1, 2)[n]
        self.p[n].wait_recv()
        self.p[n] = self.send(self.at(k, -1, slice(0, 32)), self.second(1))
        self.q[n].wait_recv()
        self.q[n] = self.send(self.at(k, 1, slice(32, 64)), self.second(-1))

    def finish(self):
        for copy in self.p + self.q:
            copy.wait_recv()

    def group(self, j):
        b = lax.rem(self.o + j + 4, 4)
        return (slice(None), b, self.half) if self.half == 0 else (b, slice(None), self.half)


class ScatterZ:
    def __init__(self, link, where, full, side, right, left, out):
        self.link, self.w, self.full, self.side = link, where, full, side
        self.right, self.left, self.out = right, left, out

    def swap(self):
        other = 1 - self.w.core
        self.pair = [
            self.link.send(self.full.at[:, other + 2 * j], self.side.at[:, j], self.w.sibling)
            for j in range(2)
        ]

    def both(self, k, half):
        to = lax.rem(self.w.z + k + NZ, NZ)
        a, j = lax.div(to, 2), lax.rem(to, 2)
        at = (a, 2 * j + self.w.core, half)
        return at, self.full[at].astype(F32) + self.side[a, j, half].astype(F32)

    def chunk(self, k):
        to = lax.rem(self.w.z + k + NZ, NZ)
        return self.full.at[lax.div(to, 2), 2 * lax.rem(to, 2) + self.w.core]

    def begin(self):
        for copy in self.pair:
            copy.wait_recv()
        self.moves = []
        for half, buf, way in ((0, self.right, 1), (1, self.left, -1)):
            at, total = self.both(4, half)
            self.full[at] = total.astype(BF)
            self.moves.append(self.link.send(self.full.at[at], buf.at[0, half], self.w.Z(way)))

    def step(self, n):
        for i, (buf, way) in enumerate(((self.right, 1), (self.left, -1))):
            self.moves[i].wait_recv()
            for half in range(2):
                at, total = self.both(way * (4 - n), half)
                if n > 1 or half == i:
                    total = total + buf[n - 1, half].astype(F32)
                self.full[at] = total.astype(BF)
            self.moves[i] = self.link.send(self.chunk(way * (4 - n)), buf.at[n], self.w.Z(way))

    def finish(self):
        for copy in self.moves:
            copy.wait_recv()
        for half in range(2):
            total = self.both(0, half)[1]
            self.out[half] = (
                total + self.right[3, half].astype(F32) + self.left[3, half].astype(F32)
            ).astype(BF)


class Where:
    def __init__(self):
        r, c = lax.axis_index("row"), lax.axis_index("col")
        self.r, self.c = r, c
        self.x, self.y = lax.div(r, NY), lax.rem(r, NY)
        self.z, self.core = lax.div(c, 2), lax.rem(c, 2)
        self.sibling = (r, 2 * self.z + 1 - self.core)

    def X(self, k):
        return (lax.rem(self.x + k + NX, NX) * NY + self.y, self.c)

    def Y(self, k):
        return (self.x * NY + lax.rem(self.y + k + NY, NY), self.c)

    def Z(self, k):
        return (self.r, lax.rem(self.z + k + NZ, NZ) * 2 + self.core)


def kernel(
    tok, go, wg, wu, wd, gm, um, dm,
    lo, ig, gg, dgt,
    t_all, g_all, tt, gt, w, wdm, p_gu, p_hg,
    ra1, ra2, sa, qa1, qa2, rb1, rb2, sb, qb1, qb2,
    ha1, ha2, hsa, hqa1, hqa2, hb1, hb2, hsb, hqb1, hqb2,
    hid, gr, silu_s, slope_s, lop, igp, lo_side, ig_side, lo_r, lo_l, ig_r, ig_l,
    send_sem, recv_sem, load_sem,
):
    where = Where()
    link = Link(send_sem, recv_sem)

    loads = [
        pltpu.make_async_copy(wg, w.at[:, 0:F], load_sem.at[0]),
        pltpu.make_async_copy(wu, w.at[:, F : 2 * F], load_sem.at[1]),
        pltpu.make_async_copy(wd, wdm, load_sem.at[2]),
    ]
    for load in loads:
        load.start()

    barrier = pltpu.get_barrier_semaphore()
    near = (where.X(1), where.X(-1), where.Y(1), where.Y(-1), where.Z(1), where.Z(-1), where.sibling)
    for device in near:
        pl.semaphore_signal(barrier, inc=1, device_id=device, device_id_type=MESH)
    pl.semaphore_wait(barrier, len(near))

    tz = GatherZ(link, where, t_all, tok)
    gz = GatherZ(link, where, g_all, go)
    tz.start()

    for load in loads:
        load.wait()

    @pl.loop(0, 4)
    def _(i):
        rows = pl.ds(pl.multiple_of(i * BLK, BLK), BLK)
        for m_ref, base in ((gm, 0), (um, F)):
            for j in range(7):
                cols = pl.ds(base + j * BLK, BLK)
                w[rows, cols] = (w[rows, cols].astype(F32) * m_ref[i, j].astype(F32)).astype(BF)

    tz.step(1)

    @pl.loop(0, 7)
    def _(i):
        rows = pl.ds(pl.multiple_of(i * BLK, BLK), BLK)
        for j in range(4):
            cols = pl.ds(j * BLK, BLK)
            wdm[rows, cols] = (wdm[rows, cols].astype(F32) * dm[i, j].astype(F32)).astype(BF)

    tz.step(2)
    tz.step(3)
    gz.start()
    tz.last()
    tz.finish()

    gu = [
        ScatterXY(link, where, 0, p_gu, (ra1, ra2, sa, qa1, qa2)),
        ScatterXY(link, where, 1, p_gu, (rb1, rb2, sb, qb1, qb2)),
    ]
    hg = [
        ScatterXY(link, where, 0, p_hg, (ha1, ha2, hsa, hqa1, hqa2)),
        ScatterXY(link, where, 1, p_hg, (hb1, hb2, hsb, hqb1, hqb2)),
    ]

    def part_gu(s, k):
        at = s.index(k)

        @pl.loop(0, 2)
        def _(n):
            cols = pl.ds(pl.multiple_of(n * F, BLK), F)
            part = dot_nn(rows_of(t_all, *at), w[:, cols])
            p_gu[(*at, slice(None), cols)] = part.astype(BF).reshape(4, 64, F)

    def part_hg(s, k):
        at = s.index(k)
        p_hg[at] = dot_nt(rows_of(g_all, *at), wdm[...]).astype(BF).reshape(4, 64, F)

    for s in gu:
        part_gu(s, 2)
        s.opposite()
    gz.step(1)
    for s in gu:
        part_gu(s, 1)
        part_gu(s, -1)
        s.raw()
    gz.step(2)
    for s in gu:
        part_gu(s, 0)
    gz.step(3)

    def transpose(src, dst):
        @pl.loop(0, 16)
        def _(c):
            block = src[lax.div(c, 4), lax.rem(c, 4)].reshape(BLK, D)
            dst[:, pl.ds(pl.multiple_of(c * BLK, BLK), BLK)] = block.T

    transpose(t_all, tt)
    gz.last()
    gz.finish()
    for s in hg:
        part_hg(s, 2)
        s.opposite()
    for s in gu:
        s.sums()
    for s in hg:
        part_hg(s, 1)
        part_hg(s, -1)
        s.raw()
    for s in hg:
        part_hg(s, 0)
    transpose(g_all, gt)
    for s in gu:
        s.middle()
    for s in hg:
        s.sums()
    for s in gu:
        s.sums2()
    for s in hg:
        s.middle()

    hid_ag = [GatherXY(link, where, h, hid) for h in range(2)]
    gr_ag = [GatherXY(link, where, h, gr) for h in range(2)]
    for h in range(2):
        gu[h].arrive()
        gate = gu[h].result(slice(0, F)).astype(BF).astype(F32)
        up = gu[h].result(slice(F, 2 * F)).astype(BF).astype(F32)
        sig = 1.0 / (1.0 + jnp.exp(-gate))
        silu = gate * sig
        silu_s[h] = silu
        slope_s[h] = up * (sig * (1.0 + gate * (1.0 - sig)))
        hid[where.x, where.y, h] = (silu * up).astype(BF)
        hid_ag[h].start()
    for s in hg:
        s.sums2()
    for a in hid_ag:
        a.near()
    for h in range(2):
        hg[h].arrive()
        hgrad = hg[h].result(slice(0, F))
        gr[where.x, where.y, h, :, 0:F] = (hgrad * slope_s[h]).astype(BF)
        gr[where.x, where.y, h, :, F : 2 * F] = (hgrad * silu_s[h]).astype(BF)
        gr_ag[h].start()
    for a in hid_ag:
        a.far()
    for n in range(2):
        for a in hid_ag:
            a.relay(n)
    for a in gr_ag:
        a.near()
    for n in range(2, 4):
        for a in hid_ag:
            a.relay(n)
    for a in gr_ag:
        a.far()
    for a in hid_ag:
        a.finish()

    lz = ScatterZ(link, where, lop, lo_side, lo_r, lo_l, lo)
    iz = ScatterZ(link, where, igp, ig_side, ig_r, ig_l, ig)

    def out_part(a):
        @pl.loop(0, 4)
        def _(j):
            b = j
            at = (slice(None), b, a.half) if a.half == 0 else (b, slice(None), a.half)
            lop[at] = dot_nn(rows_of(hid, *at), wdm[...]).astype(BF).reshape(4, 64, D)

    def in_part(a, j):
        at = a.group(j)
        igp[at] = dot_nt(rows_of(gr, *at), w[...]).astype(BF).reshape(4, 64, D)

    out_part(hid_ag[0])
    for a in gr_ag:
        a.relay(0)
    out_part(hid_ag[1])
    lz.swap()
    for a in gr_ag:
        in_part(a, 0)
    lz.begin()
    for a in gr_ag:
        a.relay(1)
    lz.step(1)

    @pl.loop(0, 7)
    def _(n):
        cols = pl.ds(pl.multiple_of(n * BLK, BLK), BLK)
        right = hid[:, :, :, :, cols].reshape(2048, BLK)
        dgt[:, cols] = dot_nn(gt[...], right).astype(BF)

    lz.step(2)
    for a in gr_ag:
        a.relay(2)
    lz.step(3)
    for a in gr_ag:
        a.relay(3)
    lz.finish()
    for a in gr_ag:
        in_part(a, -1)
        in_part(a, 1)
    for a in gr_ag:
        a.finish()
        in_part(a, 2)
    iz.swap()

    def weight_part(first, last):
        @pl.loop(first, last)
        def _(n):
            cols = pl.ds(pl.multiple_of(n * 256, 256), 256)
            right = gr[:, :, :, :, cols].reshape(2048, 256)
            gg[:, cols] = dot_nn(tt[...], right).astype(BF)

    weight_part(0, 2)
    iz.begin()
    weight_part(2, 4)
    iz.step(1)
    weight_part(4, 6)
    iz.step(2)
    weight_part(6, 7)
    iz.step(3)
    iz.finish()
    link.drain()


def scatter_bufs(n):
    return [
        pltpu.VMEM((2, 2, 64, n), BF),
        pltpu.VMEM((2, 4, 64, n), BF),
        pltpu.VMEM((4, 64, n), BF),
        pltpu.VMEM((2, 32, n), BF),
        pltpu.VMEM((2, 64, n), BF),
    ]


def expand_mask(mask_tile, tile):
    blocks_a, blocks_b = mask_tile.shape
    scaled = mask_tile.astype(tile.dtype)[:, None, :, None]
    return (tile.reshape(blocks_a, BLK, blocks_b, BLK) * scaled).reshape(tile.shape)


def body(tokens, grad_out, gate_weight, up_weight, down_weight, gate_mask, up_mask, down_mask):
    vmem = pl.BlockSpec(memory_space=pltpu.VMEM)
    smem = pl.BlockSpec(memory_space=pltpu.SMEM)
    anywhere = pl.BlockSpec(memory_space=pl.ANY)
    chunks = (4, 4, 2, 64)
    lo, ig, gg, dgt = pl.pallas_call(
        kernel,
        out_shape=(
            jax.ShapeDtypeStruct((2, 64, D), BF),
            jax.ShapeDtypeStruct((2, 64, D), BF),
            jax.ShapeDtypeStruct((D, 2 * F), BF),
            jax.ShapeDtypeStruct((D, F), BF),
        ),
        in_specs=[vmem, vmem, anywhere, anywhere, anywhere, smem, smem, smem],
        out_specs=(vmem, vmem, vmem, vmem),
        scratch_shapes=[
            pltpu.VMEM((*chunks, D), BF),
            pltpu.VMEM((*chunks, D), BF),
            pltpu.VMEM((D, 2048), BF),
            pltpu.VMEM((D, 2048), BF),
            pltpu.VMEM((D, 2 * F), BF),
            pltpu.VMEM((F, D), BF),
            pltpu.VMEM((*chunks, 2 * F), BF),
            pltpu.VMEM((*chunks, F), BF),
            *scatter_bufs(2 * F), *scatter_bufs(2 * F),
            *scatter_bufs(F), *scatter_bufs(F),
            pltpu.VMEM((*chunks, F), BF),
            pltpu.VMEM((*chunks, 2 * F), BF),
            pltpu.VMEM((2, 64, F), F32),
            pltpu.VMEM((2, 64, F), F32),
            pltpu.VMEM((*chunks, D), BF),
            pltpu.VMEM((*chunks, D), BF),
            pltpu.VMEM((4, 2, 2, 64, D), BF),
            pltpu.VMEM((4, 2, 2, 64, D), BF),
            *[pltpu.VMEM((4, 2, 64, D), BF)] * 4,
            pltpu.SemaphoreType.DMA((NSEM,)),
            pltpu.SemaphoreType.DMA((NSEM,)),
            pltpu.SemaphoreType.DMA((3,)),
        ],
        compiler_params=pltpu.CompilerParams(
            collective_id=0, has_side_effects=True, vmem_limit_bytes=63 * 2**20
        ),
        cost_estimate=pl.CostEstimate(flops=2 * 9 * 2048 * D * F, bytes_accessed=8 * 2**20, transcendentals=0),
    )(
        tokens.reshape(2, 64, D), grad_out.reshape(2, 64, D), gate_weight, up_weight, down_weight,
        gate_mask, up_mask, down_mask,
    )
    return (
        lo.reshape(BLK, D),
        ig.reshape(BLK, D),
        expand_mask(gate_mask, gg[:, :F]),
        expand_mask(up_mask, gg[:, F:]),
        expand_mask(down_mask, dgt.T),
    )


def solution(mesh):
    wide, tall = P("row", "col"), P("col", "row")
    return jax.shard_map(
        body,
        mesh=mesh,
        in_specs=(tall, tall, wide, wide, tall, wide, wide, tall),
        out_specs=(tall, tall, wide, wide, tall),
        check_vma=False,
    )
```

time: 540 us -> 196 us (0.36)
  waiting for transfers between devices: 450 us -> 0 us
  Pallas kernels: 0 us -> 183 us
  matrix products: 38.5 us -> 0 us
  local copies, waits for them, and re-layouts: 27.5 us -> 7.88 us
  between operations: 14.3 us -> 0.77 us
    all_gather x4 -> x0, waiting for transfers between devices: 198 us -> none  [the longest x1 74.3 us: body(): grads_all = lax.all_gather(grads_own, 'row', axis=0, tiled=True)]
    pallas_call x0 -> x1, Pallas kernels: none -> 183 us  [body(): pl.pallas_call(kernel, out_shape=(jax.ShapeDtypeStruct((2, 64, D), BF), j...]
    unnamed x10 -> x0, waiting for transfers between devices: 156 us -> none
    reduce_scatter x2 -> x0, waiting for transfers between devices: 96.2 us -> none  [the longest x1 61.1 us: body(): lax.psum_scatter(lax.dot_general(grad_rows, gate_up_w, (((1,), (1,)), (()...]
    dot_general x6 -> x0, matrix products: 38.5 us -> none  [the longest x1 8.88 us: body(): jnp.dot(token_cols, gate_up_w, preferred_element_type=jnp.float32)]
    unnamed x31 -> x19, local copies, waits for them, and re-layouts: 24 us -> 4.85 us
  transfers between devices with their start and end apart: 8 -> 0, of which waited for: 8 -> 0; matrix products, arithmetic and copies ran while one was open for 12% -> 0% of each run, Pallas kernels for 0% -> 0%
where the time goes in v1:
time: 196 us; the launch traced here: 194 us
  Pallas kernels  183 us (93%)
  local copies, waits for them, and re-layouts  7.88 us (4%)
  other arithmetic  3 us (2%)
    pallas_call x1, Pallas kernels, body(): pl.pallas_call(kernel, out_shape=(jax.ShapeDtypeStruct((2, 64, D), BF), j...  183 us
    unnamed x19, local copies, waits for them, and re-layouts  4.85 us

profile of v1, /device:TPU:32, one launch (start us, length us, event | category | flops | bytes accessed | tf_op | source)
XLA Modules:
  0.0 194.4 jit_solution(17223672390079213550)
XLA Ops:
  0.6 1.4 copy.15.dm
  2.0 0.0 copy-start.4
  2.0 182.7 %shard_map.119 = (bf16[2,64,512]{2,1,0:T(8,128)(2,1)}, bf16[2,64,512]{2,1,0:T(8,128)(2,1)}, bf16[512,1792]{1,0:T(8,128)(2,1)}, bf16[512,896]{1,0:T(8,128)(2,1)}) custom-call(bf16[2,64,512]{2,1,0:T(8,128)(2,1)} %bitcast.33, bf16[2,64,512]{2,1,0:T(8,128)(2,1)} %bitcast.34, bf16[512,896]{1,0:T(8,128)(2,1)} %wg.1, bf16[512,896]{1,0:T(8,128)(2,1)} %wu.1, ...), custom_call_target="tpu_custom_call" | custom-call | flops 16911433728 | bytes 8388608 | tf_op jit(solution)/shard_map/pallas_call | solution.py:528
  184.7 0.0 copy-done.4
  184.7 0.1 copy.16
  184.8 0.3 mul.33
  185.2 0.0 copy-start.5
  185.2 0.2 copy.31
  185.3 0.6 copy.17
  185.9 0.0 copy-done.5
  186.0 0.1 copy.18
  186.1 0.3 mul.36
  186.4 0.2 copy.30
  186.5 0.6 copy.19
  187.2 0.0 copy-start.3
  187.2 2.9 %slice_multiply_fusion = (bf16[512,896]{1,0:T(8,128)(2,1)}, bf16[512,896]{1,0:T(8,128)(2,1)}) fusion(bf16[512,896]{1,0:T(8,128)(2,1)S(1)} %copy.19, bf16[512,1792]{1,0:T(8,128)(2,1)} %get-tuple-element.11, bf16[512,896]{1,0:T(8,128)(2,1)S(1)} %copy.17), kind=kLoop, calls=%fused_computation.4 | loop fusion | flops 917504 | bytes 5505024 | tf_op jit(solution)/shard_map/mul | solution.py:520
  190.1 0.0 copy-done.3
  190.1 0.1 copy.20
  190.2 0.3 mul.39
  190.5 0.0 copy-start
  190.5 0.2 copy.29
  190.7 0.6 copy.21
  191.3 0.4 copy-done
  191.7 0.0 copy-start.2
  191.7 0.0 copy-start.1
  191.7 0.1 bitcast_multiply_fusion
  191.8 1.3 copy.22
  193.1 0.0 copy-done.2
  193.1 0.7 copy.34
  193.7 0.0 copy-done.1
  193.7 0.7 copy.35
  (3 shorter events, 0.0 us)
Async XLA Ops:
  2.0 182.7 %copy-start.4 = (s32[4,7]{1,0:T(4,128)S(1)}, s32[4,7]{1,0:T(4,128)}, u32[]{:S(2)}) copy-start(s32[4,7]{1,0:T(4,128)} %gm.1) | copy-start | bytes 340
  185.2 0.8 copy-start.5
  187.2 2.9 %copy-start.3 = (s32[7,4]{0,1:T(4,128)S(1)}, s32[7,4]{0,1:T(4,128)}, u32[]{:S(2)}) copy-start(s32[7,4]{0,1:T(4,128)} %param.15) | copy-start | bytes 340
  190.5 1.2 copy-start
  191.7 1.4 copy-start.2
  191.7 2.1 %copy-start.1 = (bf16[2,64,512]{2,1,0:T(8,128)(2,1)S(1)}, bf16[2,64,512]{2,1,0:T(8,128)(2,1)}, u32[]{:S(2)}) copy-start(bf16[2,64,512]{2,1,0:T(8,128)(2,1)} %get-tuple-element.10) | copy-start | bytes 393220

commit v2 on v1

--- a/solution.py
+++ b/solution.py
@@ -11,7 +11,7 @@
 D = 512
 F32, BF = jnp.float32, jnp.bfloat16
 MESH = pl.DeviceIdType.MESH
-NSEM = 200
+NSEM = 240
 
 
 def rows_of(ref, *lead):
@@ -49,29 +49,38 @@
 class GatherZ:
     def __init__(self, link, where, full, own):
         self.link, self.w, self.full, self.own = link, where, full, own
+        self.moves = {}
 
     def slot(self, k, *half):
         chunk = lax.rem(self.w.z + k + NZ, NZ) * 2 + self.w.core
         return self.full.at[(lax.div(chunk, 4), lax.rem(chunk, 4), *half)]
 
+    def move(self, way, k, half):
+        ref = self.slot(k, half)
+        self.moves[way, half] = self.link.send(ref, ref, self.w.Z(way))
+
     def start(self):
         own = self.slot(0)
         own[...] = self.own[...]
-        self.right = [self.link.send(own, own, self.w.Z(1))]
-        self.left = [self.link.send(own, own, self.w.Z(-1))]
+        for half in range(2):
+            for way in (1, -1):
+                self.move(way, 0, half if way == 1 else 1 - half)
         self.side = [self.link.send(own, own, self.w.sibling)]
 
     def step(self, k):
-        for copies, sign, half in ((self.right, -1, 0), (self.left, 1, 1)):
-            copies[k - 1].wait_recv()
-            got = self.slot(sign * k)
-            on = got if k < 3 else self.slot(sign * k, half)
-            copies.append(self.link.send(on, on, self.w.Z(-sign)))
+        for turn in range(2):
+            for way in (1, -1):
+                half = turn if way == 1 else 1 - turn
+                self.moves[way, half].wait_recv()
+                if k < 3 or turn == 0:
+                    self.move(way, -way * k, half)
+        for way in (1, -1):
+            got = self.slot(-way * k)
             self.side.append(self.link.send(got, got, self.w.sibling))
 
     def last(self):
-        self.right[3].wait_recv()
-        self.left[3].wait_recv()
+        self.moves[1, 0].wait_recv()
+        self.moves[-1, 1].wait_recv()
         got = self.slot(4)
         self.side.append(self.link.send(got, got, self.w.sibling))
 
@@ -187,13 +196,10 @@
         self.b_p = self.send(self.at(-1, 0, slice(0, 32)), self.first(1))
         self.a_m.wait_recv()
         self.b_m = self.send(self.at(1, 0, slice(32, 64)), self.first(-1))
-        self.across(-1)
-        self.across(1)
 
     def far(self):
         self.b_p.wait_recv()
         self.b_m.wait_recv()
-        self.across(2)
 
     def relay(self, n):
         k = (0, -1, 1, 2)[n]
@@ -214,7 +220,8 @@
 class ScatterZ:
     def __init__(self, link, where, full, side, right, left, out):
         self.link, self.w, self.full, self.side = link, where, full, side
-        self.right, self.left, self.out = right, left, out
+        self.bufs, self.out = {1: right, -1: left}, out
+        self.moves = {}
 
     def swap(self):
         other = 1 - self.w.core
@@ -229,37 +236,36 @@
         at = (a, 2 * j + self.w.core, half)
         return at, self.full[at].astype(F32) + self.side[a, j, half].astype(F32)
 
-    def chunk(self, k):
-        to = lax.rem(self.w.z + k + NZ, NZ)
-        return self.full.at[lax.div(to, 2), 2 * lax.rem(to, 2) + self.w.core]
+    def move(self, way, n, half, arrived):
+        at, total = self.both(way * (4 - n), half)
+        if arrived:
+            self.moves[way, half].wait_recv()
+            total = total + self.bufs[way][n - 1, half].astype(F32)
+        self.full[at] = total.astype(BF)
+        self.moves[way, half] = self.link.send(self.full.at[at], self.bufs[way].at[n, half], self.w.Z(way))
 
     def begin(self):
         for copy in self.pair:
             copy.wait_recv()
-        self.moves = []
-        for half, buf, way in ((0, self.right, 1), (1, self.left, -1)):
-            at, total = self.both(4, half)
-            self.full[at] = total.astype(BF)
-            self.moves.append(self.link.send(self.full.at[at], buf.at[0, half], self.w.Z(way)))
+        for way in (1, -1):
+            self.move(way, 0, 0 if way == 1 else 1, False)
+        for way in (1, -1):
+            self.move(way, 1, 1 if way == 1 else 0, False)
 
     def step(self, n):
-        for i, (buf, way) in enumerate(((self.right, 1), (self.left, -1))):
-            self.moves[i].wait_recv()
-            for half in range(2):
-                at, total = self.both(way * (4 - n), half)
-                if n > 1 or half == i:
-                    total = total + buf[n - 1, half].astype(F32)
-                self.full[at] = total.astype(BF)
-            self.moves[i] = self.link.send(self.chunk(way * (4 - n)), buf.at[n], self.w.Z(way))
+        for way in (1, -1):
+            self.move(way, n, 0 if way == 1 else 1, True)
+        if n < 3:
+            for way in (1, -1):
+                self.move(way, n + 1, 1 if way == 1 else 0, True)
 
     def finish(self):
-        for copy in self.moves:
-            copy.wait_recv()
         for half in range(2):
             total = self.both(0, half)[1]
-            self.out[half] = (
-                total + self.right[3, half].astype(F32) + self.left[3, half].astype(F32)
-            ).astype(BF)
+            for way in (1, -1) if half == 1 else (-1, 1):
+                self.moves[way, half].wait_recv()
+                total = total + self.bufs[way][3, half].astype(F32)
+            self.out[half] = total.astype(BF)
 
 
 class Where:
@@ -282,7 +288,7 @@
 
 def kernel(
     tok, go, wg, wu, wd, gm, um, dm,
-    lo, ig, gg, dgt,
+    lo, ig, gg, ug, dg,
     t_all, g_all, tt, gt, w, wdm, p_gu, p_hg,
     ra1, ra2, sa, qa1, qa2, rb1, rb2, sb, qb1, qb2,
     ha1, ha2, hsa, hqa1, hqa2, hb1, hb2, hsb, hqb1, hqb2,
@@ -357,6 +363,12 @@
     def part_hg(s, k):
         at = s.index(k)
         p_hg[at] = dot_nt(rows_of(g_all, *at), wdm[...]).astype(BF).reshape(4, 64, F)
+
+    def transpose(src, dst, first, last):
+        @pl.loop(first, last)
+        def _(c):
+            block = src[lax.div(c, 4), lax.rem(c, 4)].reshape(BLK, D)
+            dst[:, pl.ds(pl.multiple_of(c * BLK, BLK), BLK)] = block.T
 
     for s in gu:
         part_gu(s, 2)
@@ -367,17 +379,9 @@
         part_gu(s, -1)
         s.raw()
     gz.step(2)
-    for s in gu:
-        part_gu(s, 0)
+    part_gu(gu[0], 0)
     gz.step(3)
-
-    def transpose(src, dst):
-        @pl.loop(0, 16)
-        def _(c):
-            block = src[lax.div(c, 4), lax.rem(c, 4)].reshape(BLK, D)
-            dst[:, pl.ds(pl.multiple_of(c * BLK, BLK), BLK)] = block.T
-
-    transpose(t_all, tt)
+    part_gu(gu[1], 0)
     gz.last()
     gz.finish()
     for s in hg:
@@ -391,11 +395,12 @@
         s.raw()
     for s in hg:
         part_hg(s, 0)
-    transpose(g_all, gt)
+    transpose(t_all, tt, 0, 16)
+    for s in hg:
+        s.sums()
     for s in gu:
         s.middle()
-    for s in hg:
-        s.sums()
+    transpose(g_all, gt, 0, 16)
     for s in gu:
         s.sums2()
     for s in hg:
@@ -413,10 +418,38 @@
         slope_s[h] = up * (sig * (1.0 + gate * (1.0 - sig)))
         hid[where.x, where.y, h] = (silu * up).astype(BF)
         hid_ag[h].start()
+    lz = ScatterZ(link, where, lop, lo_side, lo_r, lo_l, lo)
+    iz = ScatterZ(link, where, igp, ig_side, ig_r, ig_l, ig)
+
+    def out_part(a, first, last):
+        @pl.loop(first, last)
+        def _(j):
+            at = (slice(None), j, a.half) if a.half == 0 else (j, slice(None), a.half)
+            lop[at] = dot_nn(rows_of(hid, *at), wdm[...]).astype(BF).reshape(4, 64, D)
+
+    def in_part(a, j):
+        at = a.group(j)
+        igp[at] = dot_nt(rows_of(gr, *at), w[...]).astype(BF).reshape(4, 64, D)
+
+    def down_part(first, last):
+        @pl.loop(first, last)
+        def _(j):
+            at = pl.ds(pl.multiple_of(j * BLK, BLK), BLK)
+
+            @pl.loop(0, 7)
+            def _(i):
+                rows = pl.ds(pl.multiple_of(i * BLK, BLK), BLK)
+                right = hid[:, :, :, :, rows].reshape(2048, BLK)
+                part = dot_nn(gt[at, :], right) * dm[i, j].astype(F32)
+                dg[rows, at] = part.T.astype(BF)
+
     for s in hg:
         s.sums2()
     for a in hid_ag:
         a.near()
+    for a in hid_ag:
+        a.across(-1)
+        a.across(1)
     for h in range(2):
         hg[h].arrive()
         hgrad = hg[h].result(slice(0, F))
@@ -425,81 +458,70 @@
         gr_ag[h].start()
     for a in hid_ag:
         a.far()
-    for n in range(2):
+        a.across(2)
+    for n in range(3):
         for a in hid_ag:
             a.relay(n)
     for a in gr_ag:
         a.near()
-    for n in range(2, 4):
-        for a in hid_ag:
-            a.relay(n)
+    for a in hid_ag:
+        a.relay(3)
+    for a in gr_ag:
+        a.across(-1)
+        a.across(1)
     for a in gr_ag:
         a.far()
+        a.across(2)
     for a in hid_ag:
         a.finish()
-
-    lz = ScatterZ(link, where, lop, lo_side, lo_r, lo_l, lo)
-    iz = ScatterZ(link, where, igp, ig_side, ig_r, ig_l, ig)
-
-    def out_part(a):
-        @pl.loop(0, 4)
-        def _(j):
-            b = j
-            at = (slice(None), b, a.half) if a.half == 0 else (b, slice(None), a.half)
-            lop[at] = dot_nn(rows_of(hid, *at), wdm[...]).astype(BF).reshape(4, 64, D)
-
-    def in_part(a, j):
-        at = a.group(j)
-        igp[at] = dot_nt(rows_of(gr, *at), w[...]).astype(BF).reshape(4, 64, D)
-
-    out_part(hid_ag[0])
+    for a in hid_ag:
+        out_part(a, 0, 4)
+    lz.swap()
     for a in gr_ag:
         a.relay(0)
-    out_part(hid_ag[1])
-    lz.swap()
+    lz.begin()
     for a in gr_ag:
         in_part(a, 0)
-    lz.begin()
     for a in gr_ag:
         a.relay(1)
     lz.step(1)
-
-    @pl.loop(0, 7)
-    def _(n):
-        cols = pl.ds(pl.multiple_of(n * BLK, BLK), BLK)
-        right = hid[:, :, :, :, cols].reshape(2048, BLK)
-        dgt[:, cols] = dot_nn(gt[...], right).astype(BF)
-
+    down_part(0, 1)
+    for a in gr_ag:
+        a.relay(2)
     lz.step(2)
-    for a in gr_ag:
-        a.relay(2)
+    down_part(1, 2)
+    for a in gr_ag:
+        a.relay(3)
     lz.step(3)
-    for a in gr_ag:
-        a.relay(3)
+    down_part(2, 4)
     lz.finish()
+    for a in gr_ag:
+        a.finish()
     for a in gr_ag:
         in_part(a, -1)
         in_part(a, 1)
-    for a in gr_ag:
-        a.finish()
         in_part(a, 2)
     iz.swap()
 
-    def weight_part(first, last):
+    def weight_part(m_ref, out, base, first, last):
         @pl.loop(first, last)
-        def _(n):
-            cols = pl.ds(pl.multiple_of(n * 256, 256), 256)
-            right = gr[:, :, :, :, cols].reshape(2048, 256)
-            gg[:, cols] = dot_nn(tt[...], right).astype(BF)
-
-    weight_part(0, 2)
+        def _(j):
+            cols = pl.ds(pl.multiple_of(base + j * BLK, BLK), BLK)
+            right = gr[:, :, :, :, cols].reshape(2048, BLK)
+            part = dot_nn(tt[...], right)
+            at = pl.ds(pl.multiple_of(j * BLK, BLK), BLK)
+            for i in range(4):
+                rows = slice(i * BLK, (i + 1) * BLK)
+                out[rows, at] = (part[rows] * m_ref[i, j].astype(F32)).astype(BF)
+
     iz.begin()
-    weight_part(2, 4)
+    weight_part(gm, gg, 0, 0, 4)
     iz.step(1)
-    weight_part(4, 6)
+    weight_part(gm, gg, 0, 4, 7)
     iz.step(2)
-    weight_part(6, 7)
+    weight_part(um, ug, F, 0, 4)
     iz.step(3)
+    weight_part(um, ug, F, 4, 7)
     iz.finish()
     link.drain()
 
@@ -514,27 +536,22 @@
     ]
 
 
-def expand_mask(mask_tile, tile):
-    blocks_a, blocks_b = mask_tile.shape
-    scaled = mask_tile.astype(tile.dtype)[:, None, :, None]
-    return (tile.reshape(blocks_a, BLK, blocks_b, BLK) * scaled).reshape(tile.shape)
-
-
 def body(tokens, grad_out, gate_weight, up_weight, down_weight, gate_mask, up_mask, down_mask):
     vmem = pl.BlockSpec(memory_space=pltpu.VMEM)
     smem = pl.BlockSpec(memory_space=pltpu.SMEM)
     anywhere = pl.BlockSpec(memory_space=pl.ANY)
     chunks = (4, 4, 2, 64)
-    lo, ig, gg, dgt = pl.pallas_call(
+    lo, ig, gg, ug, dg = pl.pallas_call(
         kernel,
         out_shape=(
             jax.ShapeDtypeStruct((2, 64, D), BF),
             jax.ShapeDtypeStruct((2, 64, D), BF),
-            jax.ShapeDtypeStruct((D, 2 * F), BF),
             jax.ShapeDtypeStruct((D, F), BF),
+            jax.ShapeDtypeStruct((D, F), BF),
+            jax.ShapeDtypeStruct((F, D), BF),
         ),
         in_specs=[vmem, vmem, anywhere, anywhere, anywhere, smem, smem, smem],
-        out_specs=(vmem, vmem, vmem, vmem),
+        out_specs=(vmem,) * 5,
         scratch_shapes=[
             pltpu.VMEM((*chunks, D), BF),
             pltpu.VMEM((*chunks, D), BF),
@@ -567,13 +584,7 @@
         tokens.reshape(2, 64, D), grad_out.reshape(2, 64, D), gate_weight, up_weight, down_weight,
         gate_mask, up_mask, down_mask,
     )
-    return (
-        lo.reshape(BLK, D),
-        ig.reshape(BLK, D),
-        expand_mask(gate_mask, gg[:, :F]),
-        expand_mask(up_mask, gg[:, F:]),
-        expand_mask(down_mask, dgt.T),
-    )
+    return lo.reshape(BLK, D), ig.reshape(BLK, D), gg, ug, dg
 
 
 def solution(mesh):

time: 196 us -> 178 us (0.908)
  Pallas kernels: 183 us -> 168 us
  other arithmetic: 3 us -> 0 us
    pallas_call x1, Pallas kernels: 183 us -> 168 us  [body(): pl.pallas_call(kernel, out_shape=(jax.ShapeDtypeStruct((2, 64, D), BF), j...]
    unnamed x19 -> x14, local copies, waits for them, and re-layouts: 4.85 us -> 8.3 us
    mul x2 -> x0, other arithmetic: 2.99 us -> none  [expand_mask(): tile.reshape(blocks_a, BLK, blocks_b, BLK) * scaled]
    mul x6 -> x0, local copies, waits for them, and re-layouts: 2.71 us -> none  [expand_mask(): tile.reshape(blocks_a, BLK, blocks_b, BLK) * scaled]
where the time goes in v2:
time: 178 us; the launch traced here: 177 us
  Pallas kernels  168 us (94%)
  local copies, waits for them, and re-layouts  8.3 us (5%)
    pallas_call x1, Pallas kernels, body(): pl.pallas_call(kernel, out_shape=(jax.ShapeDtypeStruct((2, 64, D), BF), j...  168 us
    unnamed x14, local copies, waits for them, and re-layouts  8.3 us

profile of v2, /device:TPU:32, one launch (start us, length us, event | category | flops | bytes accessed | tf_op | source)
XLA Modules:
  0.0 176.7 jit_solution(7903907187534594249)
XLA Ops:
  0.6 0.0 copy-start.3
  0.6 0.7 copy-done.3
  1.3 0.7 copy.13.dm
  2.0 167.8 %shard_map.119 = (bf16[2,64,512]{2,1,0:T(8,128)(2,1)}, bf16[2,64,512]{2,1,0:T(8,128)(2,1)}, bf16[512,896]{1,0:T(8,128)(2,1)}, bf16[512,896]{1,0:T(8,128)(2,1)}, bf16[896,512]{1,0:T(8,128)(2,1)}) custom-call(bf16[2,64,512]{2,1,0:T(8,128)(2,1)} %bitcast.6, bf16[2,64,512]{2,1,0:T(8,128)(2,1)} %bitcast.7, bf16[512,896]{1,0:T(8,128)(2,1)} %wg.1, ...), custom_call_target="tpu_custom_call" | custom-call | flops 16911433728 | bytes 8388608 | tf_op jit(solution)/shard_map/pallas_call | solution.py:544
  169.8 0.0 copy-start.2
  169.8 1.6 copy.19
  171.4 0.0 copy-done.2
  171.4 0.7 copy.20
  172.1 0.0 copy-start.1
  172.1 2.3 %copy.21 = bf16[512,896]{1,0:T(8,128)(2,1)} copy(bf16[512,896]{1,0:T(8,128)(2,1)} %get-tuple-element.22) | data formatting | bytes 1835008
  174.3 0.0 copy-done.1
  174.3 0.0 copy-start
  174.3 0.9 copy.22
  175.2 0.6 copy-done
  175.8 0.9 copy.23
Async XLA Ops:
  0.6 0.7 copy-start.3
  169.8 1.6 copy-start.2
  172.1 2.3 %copy-start.1 = (bf16[512,896]{1,0:T(8,128)(2,1)S(1)}, bf16[512,896]{1,0:T(8,128)(2,1)}, u32[]{:S(2)}) copy-start(bf16[512,896]{1,0:T(8,128)(2,1)} %get-tuple-element.23) | copy-start | bytes 2752516
  174.3 1.5 copy-start

commit v3 on v2

--- a/solution.py
+++ b/solution.py
@@ -31,14 +31,18 @@
     def __init__(self, send_sem, recv_sem):
         self.send_sem, self.recv_sem, self.copies = send_sem, recv_sem, []
 
-    def send(self, src, dst, device):
+    def prepare(self, src, dst, device):
         at = len(self.copies)
         copy = pltpu.make_async_remote_copy(
             src_ref=src, dst_ref=dst, send_sem=self.send_sem.at[at], recv_sem=self.recv_sem.at[at],
             device_id=device, device_id_type=MESH,
         )
+        self.copies.append(copy)
+        return copy
+
+    def send(self, src, dst, device):
+        copy = self.prepare(src, dst, device)
         copy.start()
-        self.copies.append(copy)
         return copy
 
     def drain(self):
@@ -84,8 +88,8 @@
         got = self.slot(4)
         self.side.append(self.link.send(got, got, self.w.sibling))
 
-    def finish(self):
-        for copy in self.side:
+    def ready(self, first, last):
+        for copy in self.side[first:last]:
             copy.wait_recv()
 
 
@@ -93,43 +97,56 @@
     def __init__(self, link, where, half, full, bufs):
         self.link, self.half, self.full = link, half, full
         self.r1, self.r2, self.s, self.q1, self.q2 = bufs
-        if half == 0:
-            self.m, self.o, self.first, self.second = where.x, where.y, where.X, where.Y
-        else:
-            self.m, self.o, self.first, self.second = where.y, where.x, where.Y, where.X
-
-    def index(self, k, *other):
-        d = lax.rem(self.m + k + 4, 4)
-        o = other[0] if other else slice(None)
-        return (d, o, self.half) if self.half == 0 else (o, d, self.half)
-
-    def opposite(self):
-        lo, hi = (self.full.at[self.index(2, slice(a, a + 2))] for a in (0, 2))
-        self.a_p = self.link.send(lo, self.r1.at[0], self.first(1))
-        self.a_m = self.link.send(hi, self.r1.at[1], self.first(-1))
-
-    def raw(self):
-        hi = self.full.at[self.index(1, slice(2, 4))]
-        lo = self.full.at[self.index(-1, slice(0, 2))]
-        self.b_p = self.link.send(hi, self.r2.at[0, 2:4], self.first(1))
-        self.b_m = self.link.send(lo, self.r2.at[1, 0:2], self.first(-1))
-
-    def sums(self):
-        self.a_p.wait_recv()
-        for i in range(2):
-            at = self.index(1, i)
-            self.full[at] = (self.full[at].astype(F32) + self.r1[0, i].astype(F32)).astype(BF)
-        src = self.full.at[self.index(1, slice(0, 2))]
-        self.c_p = self.link.send(src, self.r2.at[0, 0:2], self.first(1))
-        self.a_m.wait_recv()
-        for i in range(2):
-            at = self.index(-1, i + 2)
-            self.full[at] = (self.full[at].astype(F32) + self.r1[1, i].astype(F32)).astype(BF)
-        src = self.full.at[self.index(-1, slice(2, 4))]
-        self.c_m = self.link.send(src, self.r2.at[1, 2:4], self.first(-1))
+        self.m, self.o, self.first, self.second = where.order(half)
+        lo, hi = slice(0, 2), slice(2, 4)
+        prepare = self.link.prepare
+        self.far = [
+            prepare(self.part(2, lo), self.r1.at[0], self.first(1)),
+            prepare(self.part(2, hi), self.r1.at[1], self.first(-1)),
+        ]
+        self.plain = [
+            prepare(self.part(1, hi), self.r2.at[0, hi], self.first(1)),
+            prepare(self.part(-1, lo), self.r2.at[1, lo], self.first(-1)),
+        ]
+        self.summed = [
+            prepare(self.part(1, lo), self.r2.at[0, lo], self.first(1)),
+            prepare(self.part(-1, hi), self.r2.at[1, hi], self.first(-1)),
+        ]
+
+    def index(self, k, o):
+        return (lax.rem(self.m + k + 4, 4), o, self.half)
+
+    def part(self, k, o):
+        return self.full.at[self.index(k, o)]
+
+    def launch(self, group):
+        away = lax.rem(group - self.m + 4, 4)
+
+        @pl.when(away == 2)
+        def _():
+            for copy in self.far:
+                copy.start()
+
+        for i, k in ((0, 1), (1, 3)):
+
+            @pl.when(away == k)
+            def _():
+                self.plain[i].start()
+
+    def sums(self, group):
+        away = lax.rem(group - self.m + 4, 4)
+        for i, k, o in ((0, 1, 0), (1, 3, 2)):
+
+            @pl.when(away == k)
+            def _():
+                self.far[i].wait_recv()
+                for j in range(2):
+                    at = self.index(k, o + j)
+                    self.full[at] = (self.full[at].astype(F32) + self.r1[i, j].astype(F32)).astype(BF)
+                self.summed[i].start()
 
     def middle(self):
-        for copy in (self.b_p, self.b_m, self.c_p, self.c_m):
+        for copy in self.plain + self.summed:
             copy.wait_recv()
         for k in (2, 1, 3, 0):
             i = lax.rem(self.o + k, 4)
@@ -167,15 +184,12 @@
 class GatherXY:
     def __init__(self, link, where, half, full):
         self.link, self.half, self.full = link, half, full
-        if half == 0:
-            self.m, self.o, self.first, self.second = where.x, where.y, where.X, where.Y
-        else:
-            self.m, self.o, self.first, self.second = where.y, where.x, where.Y, where.X
+        self.m, self.o, self.first, self.second = where.order(half)
         self.p, self.q = [], []
 
     def at(self, k, j, *rows):
         a, b = lax.rem(self.m + k + 4, 4), lax.rem(self.o + j + 4, 4)
-        return self.full.at[(a, b, self.half, *rows) if self.half == 0 else (b, a, self.half, *rows)]
+        return self.full.at[(a, b, self.half, *rows)]
 
     def send(self, ref, device):
         return self.link.send(ref, ref, device)
@@ -213,8 +227,7 @@
             copy.wait_recv()
 
     def group(self, j):
-        b = lax.rem(self.o + j + 4, 4)
-        return (slice(None), b, self.half) if self.half == 0 else (b, slice(None), self.half)
+        return (slice(None), lax.rem(self.o + j + 4, 4), self.half)
 
 
 class ScatterZ:
@@ -275,6 +288,11 @@
         self.x, self.y = lax.div(r, NY), lax.rem(r, NY)
         self.z, self.core = lax.div(c, 2), lax.rem(c, 2)
         self.sibling = (r, 2 * self.z + 1 - self.core)
+        near, toward = lax.div(self.z, 2), 1 - 2 * lax.rem(self.z, 2)
+        self.groups = [lax.rem(near + k + 4, 4) for k in (0, -toward, toward, 2)]
+
+    def order(self, half):
+        return (self.x, self.y, self.X, self.Y) if half == 0 else (self.y, self.x, self.Y, self.X)
 
     def X(self, k):
         return (lax.rem(self.x + k + NX, NX) * NY + self.y, self.c)
@@ -327,21 +345,6 @@
                 cols = pl.ds(base + j * BLK, BLK)
                 w[rows, cols] = (w[rows, cols].astype(F32) * m_ref[i, j].astype(F32)).astype(BF)
 
-    tz.step(1)
-
-    @pl.loop(0, 7)
-    def _(i):
-        rows = pl.ds(pl.multiple_of(i * BLK, BLK), BLK)
-        for j in range(4):
-            cols = pl.ds(j * BLK, BLK)
-            wdm[rows, cols] = (wdm[rows, cols].astype(F32) * dm[i, j].astype(F32)).astype(BF)
-
-    tz.step(2)
-    tz.step(3)
-    gz.start()
-    tz.last()
-    tz.finish()
-
     gu = [
         ScatterXY(link, where, 0, p_gu, (ra1, ra2, sa, qa1, qa2)),
         ScatterXY(link, where, 1, p_gu, (rb1, rb2, sb, qb1, qb2)),
@@ -351,18 +354,27 @@
         ScatterXY(link, where, 1, p_hg, (hb1, hb2, hsb, hqb1, hqb2)),
     ]
 
-    def part_gu(s, k):
-        at = s.index(k)
+    def part_gu(n):
+        g = where.groups[n]
 
         @pl.loop(0, 2)
         def _(n):
             cols = pl.ds(pl.multiple_of(n * F, BLK), F)
-            part = dot_nn(rows_of(t_all, *at), w[:, cols])
-            p_gu[(*at, slice(None), cols)] = part.astype(BF).reshape(4, 64, F)
-
-    def part_hg(s, k):
-        at = s.index(k)
-        p_hg[at] = dot_nt(rows_of(g_all, *at), wdm[...]).astype(BF).reshape(4, 64, F)
+            part = dot_nn(t_all[g].reshape(512, D), w[:, cols])
+            p_gu[g, :, :, :, cols] = part.astype(BF).reshape(4, 2, 64, F)
+
+        for s in gu:
+            s.launch(g)
+
+    def part_hg(n):
+        g = where.groups[n]
+        p_hg[g] = dot_nt(g_all[g].reshape(512, D), wdm[...]).astype(BF).reshape(4, 2, 64, F)
+        for s in hg:
+            s.launch(g)
+
+    def sums(scatter, n):
+        for s in scatter:
+            s.sums(where.groups[n])
 
     def transpose(src, dst, first, last):
         @pl.loop(first, last)
@@ -370,34 +382,45 @@
             block = src[lax.div(c, 4), lax.rem(c, 4)].reshape(BLK, D)
             dst[:, pl.ds(pl.multiple_of(c * BLK, BLK), BLK)] = block.T
 
-    for s in gu:
-        part_gu(s, 2)
-        s.opposite()
+    tz.step(1)
+    tz.ready(0, 3)
+    part_gu(0)
+    tz.step(2)
+    tz.ready(3, 5)
+    part_gu(1)
+    tz.step(3)
+    gz.start()
+    tz.ready(5, 7)
+    part_gu(2)
+    tz.last()
+    tz.ready(7, 8)
+    part_gu(3)
+
+    @pl.loop(0, 7)
+    def _(i):
+        rows = pl.ds(pl.multiple_of(i * BLK, BLK), BLK)
+        for j in range(4):
+            cols = pl.ds(j * BLK, BLK)
+            wdm[rows, cols] = (wdm[rows, cols].astype(F32) * dm[i, j].astype(F32)).astype(BF)
+
     gz.step(1)
-    for s in gu:
-        part_gu(s, 1)
-        part_gu(s, -1)
-        s.raw()
+    sums(gu, 0)
     gz.step(2)
-    part_gu(gu[0], 0)
+    gz.ready(0, 3)
+    part_hg(0)
+    sums(gu, 1)
     gz.step(3)
-    part_gu(gu[1], 0)
+    gz.ready(3, 5)
+    part_hg(1)
+    sums(gu, 2)
     gz.last()
-    gz.finish()
-    for s in hg:
-        part_hg(s, 2)
-        s.opposite()
-    for s in gu:
-        s.sums()
-    for s in hg:
-        part_hg(s, 1)
-        part_hg(s, -1)
-        s.raw()
-    for s in hg:
-        part_hg(s, 0)
+    gz.ready(5, 8)
+    part_hg(2)
+    part_hg(3)
+    sums(gu, 3)
     transpose(t_all, tt, 0, 16)
-    for s in hg:
-        s.sums()
+    for n in range(4):
+        sums(hg, n)
     for s in gu:
         s.middle()
     transpose(g_all, gt, 0, 16)
@@ -416,7 +439,7 @@
         silu = gate * sig
         silu_s[h] = silu
         slope_s[h] = up * (sig * (1.0 + gate * (1.0 - sig)))
-        hid[where.x, where.y, h] = (silu * up).astype(BF)
+        hid[hid_ag[h].m, hid_ag[h].o, h] = (silu * up).astype(BF)
         hid_ag[h].start()
     lz = ScatterZ(link, where, lop, lo_side, lo_r, lo_l, lo)
     iz = ScatterZ(link, where, igp, ig_side, ig_r, ig_l, ig)
@@ -424,7 +447,7 @@
     def out_part(a, first, last):
         @pl.loop(first, last)
         def _(j):
-            at = (slice(None), j, a.half) if a.half == 0 else (j, slice(None), a.half)
+            at = (slice(None), j, a.half)
             lop[at] = dot_nn(rows_of(hid, *at), wdm[...]).astype(BF).reshape(4, 64, D)
 
     def in_part(a, j):
@@ -453,8 +476,8 @@
     for h in range(2):
         hg[h].arrive()
         hgrad = hg[h].result(slice(0, F))
-        gr[where.x, where.y, h, :, 0:F] = (hgrad * slope_s[h]).astype(BF)
-        gr[where.x, where.y, h, :, F : 2 * F] = (hgrad * silu_s[h]).astype(BF)
+        gr[gr_ag[h].m, gr_ag[h].o, h, :, 0:F] = (hgrad * slope_s[h]).astype(BF)
+        gr[gr_ag[h].m, gr_ag[h].o, h, :, F : 2 * F] = (hgrad * silu_s[h]).astype(BF)
         gr_ag[h].start()
     for a in hid_ag:
         a.far()
@@ -534,6 +557,15 @@
         pltpu.VMEM((2, 32, n), BF),
         pltpu.VMEM((2, 64, n), BF),
     ]
+
+
+def hand_over(*refs):
+    sems = refs[-1]
+    copies = [pltpu.make_async_copy(refs[i], refs[i + 5], sems.at[i]) for i in range(5)]
+    for copy in copies:
+        copy.start()
+    for copy in copies:
+        copy.wait()
 
 
 def body(tokens, grad_out, gate_weight, up_weight, down_weight, gate_mask, up_mask, down_mask):
@@ -584,7 +616,16 @@
         tokens.reshape(2, 64, D), grad_out.reshape(2, 64, D), gate_weight, up_weight, down_weight,
         gate_mask, up_mask, down_mask,
     )
-    return lo.reshape(BLK, D), ig.reshape(BLK, D), gg, ug, dg
+    hbm = pl.BlockSpec(memory_space=pltpu.HBM)
+    results = (lo.reshape(BLK, D), ig.reshape(BLK, D), gg, ug, dg)
+    return pl.pallas_call(
+        hand_over,
+        out_shape=tuple(jax.ShapeDtypeStruct(r.shape, r.dtype) for r in results),
+        in_specs=[hbm] * 5,
+        out_specs=(hbm,) * 5,
+        scratch_shapes=[pltpu.SemaphoreType.DMA((5,))],
+        compiler_params=pltpu.CompilerParams(vmem_limit_bytes=63 * 2**20),
+    )(*results)
 
 
 def solution(mesh):

time: 178 us -> 263 us (1.48)
  Pallas kernels: 168 us -> 259 us
  local copies, waits for them, and re-layouts: 8.3 us -> 1.35 us
    pallas_call x0 -> x1, Pallas kernels: none -> 92.5 us  [body(): pl.pallas_call(hand_over, out_shape=tuple((jax.ShapeDtypeStruct(r.shape,...]
    unnamed x14 -> x3, local copies, waits for them, and re-layouts: 8.3 us -> 1.35 us
where the time goes in v3:
time: 263 us; the launch traced here: 261 us
  Pallas kernels  259 us (98%)
    pallas_call x1, Pallas kernels, body(): pl.pallas_call(kernel, out_shape=(jax.ShapeDtypeStruct((2, 64, D), BF), j...  166 us
    pallas_call x1, Pallas kernels, body(): pl.pallas_call(hand_over, out_shape=tuple((jax.ShapeDtypeStruct(r.shape,...  92.5 us

profile of v3, /device:TPU:32, one launch (start us, length us, event | category | flops | bytes accessed | tf_op | source)
XLA Modules:
  0.0 261.0 jit_solution(7898032972985423029)
XLA Ops:
  0.6 0.0 copy-start
  0.6 0.7 copy-done
  1.3 0.7 copy.13.dm
  2.0 166.3 %shard_map.119 = (bf16[2,64,512]{2,1,0:T(8,128)(2,1)}, bf16[2,64,512]{2,1,0:T(8,128)(2,1)}, bf16[512,896]{1,0:T(8,128)(2,1)}, bf16[512,896]{1,0:T(8,128)(2,1)}, bf16[896,512]{1,0:T(8,128)(2,1)}) custom-call(bf16[2,64,512]{2,1,0:T(8,128)(2,1)} %bitcast.6, bf16[2,64,512]{2,1,0:T(8,128)(2,1)} %bitcast.7, bf16[512,896]{1,0:T(8,128)(2,1)} %wg.1, ...), custom_call_target="tpu_custom_call" | custom-call | flops 16911433728 | bytes 8388608 | tf_op jit(solution)/shard_map/pallas_call | solution.py:576
  168.3 92.5 %shard_map.120 = (bf16[128,512]{1,0:T(8,128)(2,1)}, bf16[128,512]{1,0:T(8,128)(2,1)}, bf16[512,896]{1,0:T(8,128)(2,1)}, bf16[512,896]{1,0:T(8,128)(2,1)}, bf16[896,512]{1,0:T(8,128)(2,1)}) custom-call(bf16[128,512]{1,0:T(8,128)(2,1)} %bitcast.4, bf16[128,512]{1,0:T(8,128)(2,1)} %bitcast.5, bf16[512,896]{1,0:T(8,128)(2,1)} %get-tuple-element.12.refs_2_, ...), custom_call_target="tpu_custom_call" | custom-call | tf_op jit(solution)/shard_map/pallas_call | solution.py:621
Async XLA Ops:
  0.6 0.7 copy-start

commit v4 on v3

--- a/solution.py
+++ b/solution.py
@@ -249,28 +249,39 @@
         at = (a, 2 * j + self.w.core, half)
         return at, self.full[at].astype(F32) + self.side[a, j, half].astype(F32)
 
-    def move(self, way, n, half, arrived):
+    def move(self, way, n, half):
         at, total = self.both(way * (4 - n), half)
-        if arrived:
+        if n >= 2:
             self.moves[way, half].wait_recv()
             total = total + self.bufs[way][n - 1, half].astype(F32)
+        if n == 2 and half == self.long(way):
+            self.skips[way].wait_recv()
+            total = total + self.bufs[way][0, half].astype(F32)
         self.full[at] = total.astype(BF)
-        self.moves[way, half] = self.link.send(self.full.at[at], self.bufs[way].at[n, half], self.w.Z(way))
+        to = self.w.Z(2 * way if n == 0 else way)
+        copy = self.link.send(self.full.at[at], self.bufs[way].at[n, half], to)
+        if n == 0:
+            self.skips[way] = copy
+        else:
+            self.moves[way, half] = copy
+
+    def long(self, way):
+        return 0 if way == 1 else 1
 
     def begin(self):
+        self.skips = {}
         for copy in self.pair:
             copy.wait_recv()
         for way in (1, -1):
-            self.move(way, 0, 0 if way == 1 else 1, False)
-        for way in (1, -1):
-            self.move(way, 1, 1 if way == 1 else 0, False)
+            self.move(way, 0, self.long(way))
+        for half in range(2):
+            for way in (1, -1):
+                self.move(way, 1, half if way == 1 else 1 - half)
 
     def step(self, n):
-        for way in (1, -1):
-            self.move(way, n, 0 if way == 1 else 1, True)
-        if n < 3:
+        for turn in range(2):
             for way in (1, -1):
-                self.move(way, n + 1, 1 if way == 1 else 0, True)
+                self.move(way, n, 1 - self.long(way) if turn == 0 else self.long(way))
 
     def finish(self):
         for half in range(2):
@@ -325,7 +336,7 @@
         load.start()
 
     barrier = pltpu.get_barrier_semaphore()
-    near = (where.X(1), where.X(-1), where.Y(1), where.Y(-1), where.Z(1), where.Z(-1), where.sibling)
+    near = (where.X(1), where.X(-1), where.Y(1), where.Y(-1), where.Z(1), where.Z(-1), where.Z(2), where.Z(-2), where.sibling)
     for device in near:
         pl.semaphore_signal(barrier, inc=1, device_id=device, device_id_type=MESH)
     pl.semaphore_wait(barrier, len(near))
@@ -401,7 +412,7 @@
         rows = pl.ds(pl.multiple_of(i * BLK, BLK), BLK)
         for j in range(4):
             cols = pl.ds(j * BLK, BLK)
-            wdm[rows, cols] = (wdm[rows, cols].astype(F32) * dm[i, j].astype(F32)).astype(BF)
+            wdm[rows, cols] = (wdm[rows, cols].astype(F32) * dm[j, i].astype(F32)).astype(BF)
 
     gz.step(1)
     sums(gu, 0)
@@ -463,7 +474,7 @@
             def _(i):
                 rows = pl.ds(pl.multiple_of(i * BLK, BLK), BLK)
                 right = hid[:, :, :, :, rows].reshape(2048, BLK)
-                part = dot_nn(gt[at, :], right) * dm[i, j].astype(F32)
+                part = dot_nn(gt[at, :], right) * dm[j, i].astype(F32)
                 dg[rows, at] = part.T.astype(BF)
 
     for s in hg:
@@ -507,7 +518,6 @@
         in_part(a, 0)
     for a in gr_ag:
         a.relay(1)
-    lz.step(1)
     down_part(0, 1)
     for a in gr_ag:
         a.relay(2)
@@ -519,10 +529,10 @@
     down_part(2, 4)
     lz.finish()
     for a in gr_ag:
-        a.finish()
-    for a in gr_ag:
         in_part(a, -1)
         in_part(a, 1)
+    for a in gr_ag:
+        a.finish()
         in_part(a, 2)
     iz.swap()
 
@@ -538,13 +548,12 @@
                 out[rows, at] = (part[rows] * m_ref[i, j].astype(F32)).astype(BF)
 
     iz.begin()
-    weight_part(gm, gg, 0, 0, 4)
-    iz.step(1)
-    weight_part(gm, gg, 0, 4, 7)
+    weight_part(gm, gg, 0, 0, 5)
     iz.step(2)
-    weight_part(um, ug, F, 0, 4)
+    weight_part(gm, gg, 0, 5, 7)
+    weight_part(um, ug, F, 0, 3)
     iz.step(3)
-    weight_part(um, ug, F, 4, 7)
+    weight_part(um, ug, F, 3, 7)
     iz.finish()
     link.drain()
 
@@ -560,11 +569,15 @@
 
 
 def hand_over(*refs):
-    sems = refs[-1]
-    copies = [pltpu.make_async_copy(refs[i], refs[i + 5], sems.at[i]) for i in range(5)]
-    for copy in copies:
+    ins, outs, bufs, sems = refs[:5], refs[5:10], refs[10:15], refs[15]
+    first = [pltpu.make_async_copy(ins[i], bufs[i], sems.at[0, i]) for i in range(5)]
+    second = [pltpu.make_async_copy(bufs[i], outs[i], sems.at[1, i]) for i in range(5)]
+    for copy in first:
         copy.start()
-    for copy in copies:
+    for i in range(5):
+        first[i].wait()
+        second[i].start()
+    for copy in second:
         copy.wait()
 
 
@@ -614,7 +627,7 @@
         cost_estimate=pl.CostEstimate(flops=2 * 9 * 2048 * D * F, bytes_accessed=8 * 2**20, transcendentals=0),
     )(
         tokens.reshape(2, 64, D), grad_out.reshape(2, 64, D), gate_weight, up_weight, down_weight,
-        gate_mask, up_mask, down_mask,
+        gate_mask, up_mask, down_mask.T,
     )
     hbm = pl.BlockSpec(memory_space=pltpu.HBM)
     results = (lo.reshape(BLK, D), ig.reshape(BLK, D), gg, ug, dg)
@@ -623,7 +636,7 @@
         out_shape=tuple(jax.ShapeDtypeStruct(r.shape, r.dtype) for r in results),
         in_specs=[hbm] * 5,
         out_specs=(hbm,) * 5,
-        scratch_shapes=[pltpu.SemaphoreType.DMA((5,))],
+        scratch_shapes=[*[pltpu.VMEM(r.shape, r.dtype) for r in results], pltpu.SemaphoreType.DMA((2, 5))],
         compiler_params=pltpu.CompilerParams(vmem_limit_bytes=63 * 2**20),
     )(*results)
 

time: 263 us -> 171 us (0.65)
  Pallas kernels: 259 us -> 170 us
    pallas_call x1, Pallas kernels: 92.5 us -> 2.98 us  [body(): pl.pallas_call(hand_over, out_shape=tuple((jax.ShapeDtypeStruct(r.shape,...]
where the time goes in v4:
time: 171 us
  Pallas kernels  170 us (99%)
    pallas_call x1, Pallas kernels, body(): pl.pallas_call(kernel, out_shape=(jax.ShapeDtypeStruct((2, 64, D), BF), j...  167 us

profile of v4, /device:TPU:32, one launch (start us, length us, event | category | flops | bytes accessed | tf_op | source)
XLA Modules:
  0.0 170.5 jit_solution(7106232858097264798)
XLA Ops:
  0.6 166.7 %shard_map.119 = (bf16[2,64,512]{2,1,0:T(8,128)(2,1)}, bf16[2,64,512]{2,1,0:T(8,128)(2,1)}, bf16[512,896]{1,0:T(8,128)(2,1)}, bf16[512,896]{1,0:T(8,128)(2,1)}, bf16[896,512]{1,0:T(8,128)(2,1)}) custom-call(bf16[2,64,512]{2,1,0:T(8,128)(2,1)} %bitcast.7, bf16[2,64,512]{2,1,0:T(8,128)(2,1)} %bitcast.8, bf16[512,896]{1,0:T(8,128)(2,1)} %wg.1, ...), custom_call_target="tpu_custom_call" | custom-call | flops 16911433728 | bytes 8388608 | tf_op jit(solution)/shard_map/pallas_call | solution.py:589
  167.4 3.0 %shard_map.120 = (bf16[128,512]{1,0:T(8,128)(2,1)}, bf16[128,512]{1,0:T(8,128)(2,1)}, bf16[512,896]{1,0:T(8,128)(2,1)}, bf16[512,896]{1,0:T(8,128)(2,1)}, bf16[896,512]{1,0:T(8,128)(2,1)}) custom-call(bf16[128,512]{1,0:T(8,128)(2,1)} %bitcast.5, bf16[128,512]{1,0:T(8,128)(2,1)} %bitcast.6, bf16[512,896]{1,0:T(8,128)(2,1)} %get-tuple-element.12.refs_2_, ...), custom_call_target="tpu_custom_call" | custom-call | tf_op jit(solution)/shard_map/pallas_call | solution.py:634

commit v5 on v4

--- a/solution.py
+++ b/solution.py
@@ -416,24 +416,25 @@
 
     gz.step(1)
     sums(gu, 0)
+    sums(gu, 1)
     gz.step(2)
     gz.ready(0, 3)
     part_hg(0)
-    sums(gu, 1)
+    sums(gu, 2)
     gz.step(3)
     gz.ready(3, 5)
     part_hg(1)
-    sums(gu, 2)
+    gz.ready(5, 7)
+    part_hg(2)
+    sums(gu, 3)
     gz.last()
-    gz.ready(5, 8)
-    part_hg(2)
+    gz.ready(7, 8)
     part_hg(3)
-    sums(gu, 3)
-    transpose(t_all, tt, 0, 16)
     for n in range(4):
         sums(hg, n)
     for s in gu:
         s.middle()
+    transpose(t_all, tt, 0, 16)
     transpose(g_all, gt, 0, 16)
     for s in gu:
         s.sums2()
@@ -455,27 +456,30 @@
     lz = ScatterZ(link, where, lop, lo_side, lo_r, lo_l, lo)
     iz = ScatterZ(link, where, igp, ig_side, ig_r, ig_l, ig)
 
-    def out_part(a, first, last):
-        @pl.loop(first, last)
-        def _(j):
-            at = (slice(None), j, a.half)
-            lop[at] = dot_nn(rows_of(hid, *at), wdm[...]).astype(BF).reshape(4, 64, D)
+    def out_part():
+        @pl.loop(0, 4)
+        def _(d):
+            lop[d] = dot_nn(hid[d].reshape(512, F), wdm[...]).astype(BF).reshape(4, 2, 64, D)
 
     def in_part(a, j):
         at = a.group(j)
         igp[at] = dot_nt(rows_of(gr, *at), w[...]).astype(BF).reshape(4, 64, D)
 
+    def down_tile(first, width):
+        right = hid[:, :, :, :, pl.ds(first, width)].reshape(2048, width)
+        part = dot_nn(gt[...], right)
+        for i in range(width // BLK):
+            for j in range(4):
+                block = part[j * BLK : (j + 1) * BLK, i * BLK : (i + 1) * BLK] * dm[j, first // BLK + i].astype(F32)
+                dg[pl.ds(first + i * BLK, BLK), j * BLK : (j + 1) * BLK] = block.T.astype(BF)
+
     def down_part(first, last):
-        @pl.loop(first, last)
-        def _(j):
-            at = pl.ds(pl.multiple_of(j * BLK, BLK), BLK)
-
-            @pl.loop(0, 7)
-            def _(i):
-                rows = pl.ds(pl.multiple_of(i * BLK, BLK), BLK)
-                right = hid[:, :, :, :, rows].reshape(2048, BLK)
-                part = dot_nn(gt[at, :], right) * dm[j, i].astype(F32)
-                dg[rows, at] = part.T.astype(BF)
+        @pl.loop(first, min(last, 3))
+        def _(n):
+            down_tile(pl.multiple_of(n * 256, 256), 256)
+
+        if last == 4:
+            down_tile(768, BLK)
 
     for s in hg:
         s.sums2()
@@ -504,56 +508,62 @@
         a.across(-1)
         a.across(1)
     for a in gr_ag:
+        a.relay(0)
+    for a in gr_ag:
         a.far()
         a.across(2)
     for a in hid_ag:
         a.finish()
-    for a in hid_ag:
-        out_part(a, 0, 4)
+    for a in gr_ag:
+        a.relay(1)
+    out_part()
     lz.swap()
-    for a in gr_ag:
-        a.relay(0)
+    down_part(0, 1)
+    for a in gr_ag:
+        a.relay(2)
     lz.begin()
     for a in gr_ag:
         in_part(a, 0)
-    for a in gr_ag:
-        a.relay(1)
-    down_part(0, 1)
-    for a in gr_ag:
-        a.relay(2)
-    lz.step(2)
     down_part(1, 2)
     for a in gr_ag:
         a.relay(3)
-    lz.step(3)
-    down_part(2, 4)
-    lz.finish()
     for a in gr_ag:
         in_part(a, -1)
         in_part(a, 1)
+    lz.step(2)
+    down_part(2, 4)
     for a in gr_ag:
         a.finish()
         in_part(a, 2)
     iz.swap()
-
-    def weight_part(m_ref, out, base, first, last):
-        @pl.loop(first, last)
-        def _(j):
-            cols = pl.ds(pl.multiple_of(base + j * BLK, BLK), BLK)
-            right = gr[:, :, :, :, cols].reshape(2048, BLK)
-            part = dot_nn(tt[...], right)
-            at = pl.ds(pl.multiple_of(j * BLK, BLK), BLK)
+    lz.step(3)
+
+    def weight_tile(m_ref, out, base, first, width):
+        right = gr[:, :, :, :, pl.ds(base + first, width)].reshape(2048, width)
+        part = dot_nn(tt[...], right)
+        for j in range(width // BLK):
+            at = pl.ds(first + j * BLK, BLK)
             for i in range(4):
                 rows = slice(i * BLK, (i + 1) * BLK)
-                out[rows, at] = (part[rows] * m_ref[i, j].astype(F32)).astype(BF)
+                live = m_ref[i, first // BLK + j].astype(F32)
+                out[rows, at] = (part[rows, j * BLK : (j + 1) * BLK] * live).astype(BF)
+
+    def weight_part(m_ref, out, base, first, last):
+        @pl.loop(min(first, 3), min(last, 3))
+        def _(n):
+            weight_tile(m_ref, out, base, pl.multiple_of(n * 256, 256), 256)
+
+        if last == 4:
+            weight_tile(m_ref, out, base, 768, BLK)
 
     iz.begin()
-    weight_part(gm, gg, 0, 0, 5)
+    weight_part(gm, gg, 0, 0, 3)
+    lz.finish()
     iz.step(2)
-    weight_part(gm, gg, 0, 5, 7)
-    weight_part(um, ug, F, 0, 3)
+    weight_part(gm, gg, 0, 3, 4)
+    weight_part(um, ug, F, 0, 2)
     iz.step(3)
-    weight_part(um, ug, F, 3, 7)
+    weight_part(um, ug, F, 2, 4)
     iz.finish()
     link.drain()
 

time: 171 us -> 170 us (level)
  no operation moved by 1% of the time
where the time goes in v5:
time: 170 us; the launch traced here: 169 us
  Pallas kernels  169 us (99%)
    pallas_call x1, Pallas kernels, body(): pl.pallas_call(kernel, out_shape=(jax.ShapeDtypeStruct((2, 64, D), BF), j...  166 us

profile of v5, /device:TPU:32, one launch (start us, length us, event | category | flops | bytes accessed | tf_op | source)
XLA Modules:
  0.0 169.4 jit_solution(5121208268137510519)
XLA Ops:
  0.6 165.7 %shard_map.119 = (bf16[2,64,512]{2,1,0:T(8,128)(2,1)}, bf16[2,64,512]{2,1,0:T(8,128)(2,1)}, bf16[512,896]{1,0:T(8,128)(2,1)}, bf16[512,896]{1,0:T(8,128)(2,1)}, bf16[896,512]{1,0:T(8,128)(2,1)}) custom-call(bf16[2,64,512]{2,1,0:T(8,128)(2,1)} %bitcast.7, bf16[2,64,512]{2,1,0:T(8,128)(2,1)} %bitcast.8, bf16[512,896]{1,0:T(8,128)(2,1)} %wg.1, ...), custom_call_target="tpu_custom_call" | custom-call | flops 16911433728 | bytes 8388608 | tf_op jit(solution)/shard_map/pallas_call | solution.py:599
  166.3 3.0 %shard_map.120 = (bf16[128,512]{1,0:T(8,128)(2,1)}, bf16[128,512]{1,0:T(8,128)(2,1)}, bf16[512,896]{1,0:T(8,128)(2,1)}, bf16[512,896]{1,0:T(8,128)(2,1)}, bf16[896,512]{1,0:T(8,128)(2,1)}) custom-call(bf16[128,512]{1,0:T(8,128)(2,1)} %bitcast.5, bf16[128,512]{1,0:T(8,128)(2,1)} %bitcast.6, bf16[512,896]{1,0:T(8,128)(2,1)} %get-tuple-element.12.refs_2_, ...), custom_call_target="tpu_custom_call" | custom-call | tf_op jit(solution)/shard_map/pallas_call | solution.py:644

commit v6 on v5

--- a/solution.py
+++ b/solution.py
@@ -148,17 +148,22 @@
     def middle(self):
         for copy in self.plain + self.summed:
             copy.wait_recv()
-        for k in (2, 1, 3, 0):
+        def total(k):
             i = lax.rem(self.o + k, 4)
             at = self.index(0, i)
             self.s[i] = (
                 self.full[at].astype(F32) + self.r2[0, i].astype(F32) + self.r2[1, i].astype(F32)
             ).astype(BF)
-        p, q, m = (lax.rem(self.o + k, 4) for k in (1, 2, 3))
+            return i
+
+        q = total(2)
         self.d_p = self.link.send(self.s.at[q, 0:32], self.q1.at[0], self.second(1))
         self.d_m = self.link.send(self.s.at[q, 32:64], self.q1.at[1], self.second(-1))
+        p = total(1)
         self.e_p = self.link.send(self.s.at[p, 32:64], self.q2.at[0, 32:64], self.second(1))
+        m = total(3)
         self.e_m = self.link.send(self.s.at[m, 0:32], self.q2.at[1, 0:32], self.second(-1))
+        total(0)
 
     def sums2(self):
         p, m = (lax.rem(self.o + k, 4) for k in (1, 3))
@@ -317,8 +322,8 @@
 
 def kernel(
     tok, go, wg, wu, wd, gm, um, dm,
-    lo, ig, gg, ug, dg,
-    t_all, g_all, tt, gt, w, wdm, p_gu, p_hg,
+    lo, ig, gg_out, ug_out, dg_out,
+    gg, ug, dg, t_all, g_all, tt, gt, w, wdm, p_gu, p_hg,
     ra1, ra2, sa, qa1, qa2, rb1, rb2, sb, qb1, qb2,
     ha1, ha2, hsa, hqa1, hqa2, hb1, hb2, hsb, hqb1, hqb2,
     hid, gr, silu_s, slope_s, lop, igp, lo_side, ig_side, lo_r, lo_l, ig_r, ig_l,
@@ -331,6 +336,10 @@
         pltpu.make_async_copy(wg, w.at[:, 0:F], load_sem.at[0]),
         pltpu.make_async_copy(wu, w.at[:, F : 2 * F], load_sem.at[1]),
         pltpu.make_async_copy(wd, wdm, load_sem.at[2]),
+    ]
+    stores = [
+        pltpu.make_async_copy(buf, out, load_sem.at[3 + i])
+        for i, (buf, out) in enumerate(((dg, dg_out), (gg, gg_out), (ug, ug_out)))
     ]
     for load in loads:
         load.start()
@@ -532,6 +541,7 @@
         in_part(a, 1)
     lz.step(2)
     down_part(2, 4)
+    stores[0].start()
     for a in gr_ag:
         a.finish()
         in_part(a, 2)
@@ -561,11 +571,15 @@
     lz.finish()
     iz.step(2)
     weight_part(gm, gg, 0, 3, 4)
+    stores[1].start()
     weight_part(um, ug, F, 0, 2)
     iz.step(3)
     weight_part(um, ug, F, 2, 4)
+    stores[2].start()
     iz.finish()
     link.drain()
+    for store in stores:
+        store.wait()
 
 
 def scatter_bufs(n):
@@ -606,8 +620,11 @@
             jax.ShapeDtypeStruct((F, D), BF),
         ),
         in_specs=[vmem, vmem, anywhere, anywhere, anywhere, smem, smem, smem],
-        out_specs=(vmem,) * 5,
+        out_specs=(vmem, vmem, anywhere, anywhere, anywhere),
         scratch_shapes=[
+            pltpu.VMEM((D, F), BF),
+            pltpu.VMEM((D, F), BF),
+            pltpu.VMEM((F, D), BF),
             pltpu.VMEM((*chunks, D), BF),
             pltpu.VMEM((*chunks, D), BF),
             pltpu.VMEM((D, 2048), BF),
@@ -629,7 +646,7 @@
             *[pltpu.VMEM((4, 2, 64, D), BF)] * 4,
             pltpu.SemaphoreType.DMA((NSEM,)),
             pltpu.SemaphoreType.DMA((NSEM,)),
-            pltpu.SemaphoreType.DMA((3,)),
+            pltpu.SemaphoreType.DMA((6,)),
         ],
         compiler_params=pltpu.CompilerParams(
             collective_id=0, has_side_effects=True, vmem_limit_bytes=63 * 2**20

time: 170 us -> 169 us (level)
  no operation moved by 1% of the time
where the time goes in v6:
time: 169 us
  Pallas kernels  168 us (99%)
    pallas_call x1, Pallas kernels, body(): pl.pallas_call(kernel, out_shape=(jax.ShapeDtypeStruct((2, 64, D), BF), j...  165 us

profile of v6, /device:TPU:32, one launch (start us, length us, event | category | flops | bytes accessed | tf_op | source)
XLA Modules:
  0.0 168.5 jit_solution(1386821240221603995)
XLA Ops:
  0.6 164.7 %shard_map.119 = (bf16[2,64,512]{2,1,0:T(8,128)(2,1)}, bf16[2,64,512]{2,1,0:T(8,128)(2,1)}, bf16[512,896]{1,0:T(8,128)(2,1)}, bf16[512,896]{1,0:T(8,128)(2,1)}, bf16[896,512]{1,0:T(8,128)(2,1)}) custom-call(bf16[2,64,512]{2,1,0:T(8,128)(2,1)} %bitcast.7, bf16[2,64,512]{2,1,0:T(8,128)(2,1)} %bitcast.8, bf16[512,896]{1,0:T(8,128)(2,1)} %wg.1, ...), custom_call_target="tpu_custom_call" | custom-call | flops 16911433728 | bytes 8388608 | tf_op jit(solution)/shard_map/pallas_call | solution.py:613
  165.4 3.0 %shard_map.120 = (bf16[128,512]{1,0:T(8,128)(2,1)}, bf16[128,512]{1,0:T(8,128)(2,1)}, bf16[512,896]{1,0:T(8,128)(2,1)}, bf16[512,896]{1,0:T(8,128)(2,1)}, bf16[896,512]{1,0:T(8,128)(2,1)}) custom-call(bf16[128,512]{1,0:T(8,128)(2,1)} %bitcast.5, bf16[128,512]{1,0:T(8,128)(2,1)} %bitcast.6, bf16[512,896]{1,0:T(8,128)(2,1)} %get-tuple-element.12.refs_2_, ...), custom_call_target="tpu_custom_call" | custom-call | tf_op jit(solution)/shard_map/pallas_call | solution.py:661
